TPU v7x, 32 devices: a whole 2x2x4 slice. The times are simulated.
32 devices in a mesh: dp: 32 (over z, y, x, core).
Axes of the slice: x: 2, y: 2, z: 4, core: 2. Of those that a mesh axis runs over, the one named last changes fastest.
Arguments:
- tokens: bfloat16 [32768, 1024], P('dp'), may hold values from -6 to 6
- cotangent: bfloat16 [32768, 1024], P('dp'), may hold values from -6 to 6
- w_qkv: bfloat16 [1024, 3072], P('dp'), may hold values from -0.1875 to 0.1875
- q_bias: bfloat16 [1024], P('dp'), may hold values from -2 to 2
- v_bias: bfloat16 [1024], P('dp'), may hold values from -2 to 2
- w_out: bfloat16 [1024, 1024], P('dp'), may hold values from -0.75 to 0.75
- out_bias: bfloat16 [1024], P('dp'), may hold values from -2 to 2
- attn_gain: bfloat16 [1024], P('dp'), may hold values from 0.5 to 1.5
- attn_shift: bfloat16 [1024], P('dp'), may hold values from -2 to 2
- w_up: bfloat16 [1024, 4096], P('dp'), may hold values from -0.1875 to 0.1875
- up_bias: bfloat16 [4096], P('dp'), may hold values from -2 to 2
- w_down: bfloat16 [4096, 1024], P('dp'), may hold values from -0.1875 to 0.1875
- down_bias: bfloat16 [1024], P('dp'), may hold values from -2 to 2
- mlp_gain: bfloat16 [1024], P('dp'), may hold values from 0.5 to 1.5
- mlp_shift: bfloat16 [1024], P('dp'), may hold values from -2 to 2
Outputs:
- layer_out: bfloat16 [32768, 1024], P('dp')
- input_grad: bfloat16 [32768, 1024], P('dp')
- w_qkv_grad: float32 [1024, 3072], P('dp')
- q_bias_grad: float32 [1024], P('dp')
- v_bias_grad: float32 [1024], P('dp')
- w_out_grad: float32 [1024, 1024], P('dp')
- out_bias_grad: float32 [1024], P('dp')
- attn_gain_grad: float32 [1024], P('dp')
- attn_shift_grad: float32 [1024], P('dp')
- w_up_grad: float32 [1024, 4096], P('dp')
- up_bias_grad: float32 [4096], P('dp')
- w_down_grad: float32 [4096, 1024], P('dp')
- down_bias_grad: float32 [1024], P('dp')
- mlp_gain_grad: float32 [1024], P('dp')
- mlp_shift_grad: float32 [1024], P('dp')
All inputs are finite; a program needn't handle non-finite values.
Results may differ from a plain program's by a relative error of at most 0.015.
Values may be sent and summed in bfloat16 or wider, within the bound.
No kernel may reach another device: no remote copies, remote signals or barrier semaphores. Data moves between devices by JAX's collectives and lax.ppermute only.
A program may use at most 256 MiB of HBM per device.

v0:
```python
import math

import jax
import jax.numpy as jnp
from jax import lax
from jax.sharding import PartitionSpec as P

HD = 64
LEN = 512


def layer_norm(value, gain, shift):
    center = value - jnp.mean(value, axis=-1, keepdims=True)
    spread = jnp.mean(center * center, axis=-1, keepdims=True)
    return center * lax.rsqrt(spread + 1e-05) * gain + shift


def gelu_exact(value):
    return jax.nn.gelu(value, approximate=False)


def attend_forward(triple):
    queries, keys_rows, values_rows = triple
    scale = 1.0 / math.sqrt(HD)
    scores = (
        jnp.einsum("qhd,khd->hqk", queries, keys_rows, preferred_element_type=jnp.float32) * scale
    )
    highest = jnp.max(scores, axis=-1, keepdims=True)
    total = jnp.sum(jnp.exp(scores - highest), axis=-1, keepdims=True)
    log_total = highest + jnp.log(total)
    probs = jnp.exp(scores - log_total).astype(jnp.bfloat16)
    context = jnp.einsum("hqk,khd->qhd", probs, values_rows, preferred_element_type=jnp.float32)
    return (context, log_total)


def attend_backward(bundle):
    queries, keys_rows, values_rows, log_total, d_context = bundle
    scale = 1.0 / math.sqrt(HD)
    scores = (
        jnp.einsum("qhd,khd->hqk", queries, keys_rows, preferred_element_type=jnp.float32) * scale
    )
    probs = jnp.exp(scores - log_total)
    d_values = jnp.einsum(
        "hqk,qhd->khd", probs.astype(jnp.bfloat16), d_context, preferred_element_type=jnp.float32
    )
    d_probs = jnp.einsum("qhd,khd->hqk", d_context, values_rows, preferred_element_type=jnp.float32)
    d_scores = probs * (d_probs - jnp.sum(probs * d_probs, axis=-1, keepdims=True))
    d_scores = d_scores.astype(jnp.bfloat16)
    d_queries = (
        jnp.einsum("hqk,khd->qhd", d_scores, keys_rows, preferred_element_type=jnp.float32) * scale
    )
    d_keys = (
        jnp.einsum("hqk,qhd->khd", d_scores, queries, preferred_element_type=jnp.float32) * scale
    )
    length = queries.shape[0]
    joined = jnp.concatenate(
        [d_queries.reshape(length, -1), d_keys.reshape(length, -1), d_values.reshape(length, -1)],
        axis=1,
    )
    return joined.astype(jnp.bfloat16)


def local(
    tokens,
    cotangent,
    w_qkv,
    q_bias,
    v_bias,
    w_out,
    out_bias,
    attn_gain,
    attn_shift,
    w_up,
    up_bias,
    w_down,
    down_bias,
    mlp_gain,
    mlp_shift,
):
    attn_set = (
        lax.all_gather(w_qkv, "dp", axis=0, tiled=True),
        lax.all_gather(q_bias, "dp", axis=0, tiled=True),
        lax.all_gather(v_bias, "dp", axis=0, tiled=True),
        lax.all_gather(w_out, "dp", axis=0, tiled=True),
        lax.all_gather(out_bias, "dp", axis=0, tiled=True),
        lax.all_gather(attn_gain, "dp", axis=0, tiled=True),
        lax.all_gather(attn_shift, "dp", axis=0, tiled=True),
    )
    mlp_set = (
        lax.all_gather(w_up, "dp", axis=0, tiled=True),
        lax.all_gather(up_bias, "dp", axis=0, tiled=True),
        lax.all_gather(w_down, "dp", axis=0, tiled=True),
        lax.all_gather(down_bias, "dp", axis=0, tiled=True),
        lax.all_gather(mlp_gain, "dp", axis=0, tiled=True),
        lax.all_gather(mlp_shift, "dp", axis=0, tiled=True),
    )
    full_qkv, full_qb, full_vb, full_out, full_ob, full_g1, full_s1 = attn_set
    full_up, full_ub, full_down, full_db, full_g2, full_s2 = mlp_set
    rows, width = tokens.shape
    count = rows // LEN
    heads = width // HD
    bias_full = jnp.concatenate([full_qb, jnp.zeros_like(full_qb), full_vb]).astype(jnp.float32)
    projected = (jnp.dot(tokens, full_qkv, preferred_element_type=jnp.float32) + bias_full).astype(
        jnp.bfloat16
    )
    queries = projected[:, :width].reshape(count, LEN, heads, HD)
    keys_rows = projected[:, width : 2 * width].reshape(count, LEN, heads, HD)
    values_rows = projected[:, 2 * width :].reshape(count, LEN, heads, HD)
    context, log_total = lax.map(attend_forward, (queries, keys_rows, values_rows))
    context = context.reshape(rows, width).astype(jnp.bfloat16)
    attn = jnp.dot(context, full_out, preferred_element_type=jnp.float32) + full_ob.astype(
        jnp.float32
    )
    inputs = tokens.astype(jnp.float32)
    gain_one = full_g1.astype(jnp.float32)
    shift_one = full_s1.astype(jnp.float32)
    first_sum = inputs + attn
    normed = layer_norm(first_sum, gain_one, shift_one)
    normed_low = normed.astype(jnp.bfloat16)
    upper = jnp.dot(normed_low, full_up, preferred_element_type=jnp.float32) + full_ub.astype(
        jnp.float32
    )
    active = gelu_exact(upper).astype(jnp.bfloat16)
    branch = jnp.dot(active, full_down, preferred_element_type=jnp.float32) + full_db.astype(
        jnp.float32
    )
    second_sum = normed + branch
    gain_two = full_g2.astype(jnp.float32)
    shift_two = full_s2.astype(jnp.float32)
    layer_out = layer_norm(second_sum, gain_two, shift_two).astype(jnp.bfloat16)
    back_up, back_down = (
        lax.all_gather(w_up, "dp", axis=0, tiled=True),
        lax.all_gather(w_down, "dp", axis=0, tiled=True),
    )
    unused, pull_two = jax.vjp(layer_norm, second_sum, gain_two, shift_two)
    d_second, d_gain_two, d_shift_two = pull_two(cotangent.astype(jnp.float32))
    d_branch = d_second.astype(jnp.bfloat16)
    d_w_down = jnp.einsum("tf,td->fd", active, d_branch, preferred_element_type=jnp.float32)
    d_down_bias = jnp.sum(d_branch.astype(jnp.float32), axis=0)
    d_active = jnp.einsum("td,fd->tf", d_branch, back_down, preferred_element_type=jnp.float32)
    unused_gelu, pull_gelu = jax.vjp(gelu_exact, upper)
    d_upper = pull_gelu(d_active)[0].astype(jnp.bfloat16)
    d_w_up = jnp.einsum("td,tf->df", normed_low, d_upper, preferred_element_type=jnp.float32)
    d_up_bias = jnp.sum(d_upper.astype(jnp.float32), axis=0)
    d_normed = (
        jnp.einsum("tf,df->td", d_upper, back_up, preferred_element_type=jnp.float32) + d_second
    )
    mlp_terms = (d_w_up, d_up_bias, d_w_down, d_down_bias, d_gain_two, d_shift_two)
    mlp_shares = (
        lax.psum_scatter(mlp_terms[0], "dp", scatter_dimension=0, tiled=True),
        lax.psum_scatter(mlp_terms[1], "dp", scatter_dimension=0, tiled=True),
        lax.psum_scatter(mlp_terms[2], "dp", scatter_dimension=0, tiled=True),
        lax.psum_scatter(mlp_terms[3], "dp", scatter_dimension=0, tiled=True),
        lax.psum_scatter(mlp_terms[4], "dp", scatter_dimension=0, tiled=True),
        lax.psum_scatter(mlp_terms[5], "dp", scatter_dimension=0, tiled=True),
    )
    back_qkv, back_out = (
        lax.all_gather(w_qkv, "dp", axis=0, tiled=True),
        lax.all_gather(w_out, "dp", axis=0, tiled=True),
    )
    unused_one, pull_one = jax.vjp(layer_norm, first_sum, gain_one, shift_one)
    d_first, d_gain_one, d_shift_one = pull_one(d_normed)
    d_attn = d_first.astype(jnp.bfloat16)
    d_w_out = jnp.einsum("te,td->ed", context, d_attn, preferred_element_type=jnp.float32)
    d_out_bias = jnp.sum(d_attn.astype(jnp.float32), axis=0)
    d_context = jnp.einsum("td,ed->te", d_attn, back_out, preferred_element_type=jnp.float32)
    d_context = d_context.astype(jnp.bfloat16).reshape(count, LEN, heads, HD)
    d_projected = lax.map(attend_backward, (queries, keys_rows, values_rows, log_total, d_context))
    d_projected = d_projected.reshape(rows, 3 * width)
    d_w_qkv = jnp.einsum("td,te->de", tokens, d_projected, preferred_element_type=jnp.float32)
    d_wide = d_projected.astype(jnp.float32)
    d_q_bias = jnp.sum(d_wide[:, :width], axis=0)
    d_v_bias = jnp.sum(d_wide[:, 2 * width :], axis=0)
    input_grad = d_first + jnp.einsum(
        "te,de->td", d_projected, back_qkv, preferred_element_type=jnp.float32
    )
    attn_terms = (d_w_qkv, d_q_bias, d_v_bias, d_w_out, d_out_bias, d_gain_one, d_shift_one)
    attn_shares = (
        lax.psum_scatter(attn_terms[0], "dp", scatter_dimension=0, tiled=True),
        lax.psum_scatter(attn_terms[1], "dp", scatter_dimension=0, tiled=True),
        lax.psum_scatter(attn_terms[2], "dp", scatter_dimension=0, tiled=True),
        lax.psum_scatter(attn_terms[3], "dp", scatter_dimension=0, tiled=True),
        lax.psum_scatter(attn_terms[4], "dp", scatter_dimension=0, tiled=True),
        lax.psum_scatter(attn_terms[5], "dp", scatter_dimension=0, tiled=True),
        lax.psum_scatter(attn_terms[6], "dp", scatter_dimension=0, tiled=True),
    )
    return (layer_out, input_grad.astype(jnp.bfloat16)) + tuple(attn_shares) + tuple(mlp_shares)


def solution(mesh):
    in_specs = (
        P("dp", None),
        P("dp", None),
        P("dp", None),
        P("dp"),
        P("dp"),
        P("dp", None),
        P("dp"),
        P("dp"),
        P("dp"),
        P("dp", None),
        P("dp"),
        P("dp", None),
        P("dp"),
        P("dp"),
        P("dp"),
    )
    out_specs = (
        P("dp", None),
        P("dp", None),
        P("dp", None),
        P("dp"),
        P("dp"),
        P("dp", None),
        P("dp"),
        P("dp"),
        P("dp"),
        P("dp", None),
        P("dp"),
        P("dp", None),
        P("dp"),
        P("dp"),
        P("dp"),
    )
    return jax.shard_map(local, mesh=mesh, in_specs=in_specs, out_specs=out_specs, check_vma=False)
```

profile of v0, /device:TPU:0, one launch (start us, length us, event | category | flops | bytes accessed | tf_op | source)
XLA Modules:
  0.0 1076.5 jit_solution(13614499304739241792)
XLA Ops:
  16.0 42.6 %all-reduce.18 = (bf16[1024]{0:T(1024)(128)(2,1)S(1)}, bf16[1024]{0:T(1024)(128)(2,1)S(1)}, bf16[1024]{0:T(1024)(128)(2,1)S(1)}, bf16[1024]{0:T(1024)(128)(2,1)S...) all-reduce(bf16[1024]{0:T(1024)(128)(2,1)S(1)} %dynamic-update-slic, ...), channel_id=1, replica_groups=mesh['dp'=32] {'dp'}, use_global_device_ids=true, to_apply=%add.2 | all-reduce | flops 8192 | bytes 32768
  59.2 40.3 %all-gather = bf16[32,1,128]{2,1,0:T(2,128)(2,1)S(1)} all-gather(bf16[1,1,128]{2,1,0:T(2,128)(2,1)S(1)} %bitcast.138), channel_id=1, replica_groups=mesh['dp'=32] {'dp'}, dimensions={0}, use_global_device_ids=true | all-gather | bytes 8448 | tf_op jit(solution)/shard_map/all_gather | solution.py:91
  103.3 9.7 add_convert_fusion.1
  147.9 57.7 %while.22 = (s32[]{:T(128)}, bf16[2,512,16,64]{1,3,2,0:T(8,128)(2,1)}, f32[2,16,512,1]{2,1,3,0:T(8,128)S(1)}, bf16[2,512,16,64]{1,3,2,0:T(8,128)(2,1)}, bf16[2,5...) while((s32[]{:T(128)}, bf16[2,512,16,64]{1,3,2,0:T(8,128)(2,1)}, ...), condition=%wide.region_3.4_spmd, body=%wide.region_0.3_spmd.sunk | while | flops 1107288064 | bytes 55838808 | solution.py:109
  148.1 9.3 multiply_reduce_fusion.8
  157.4 8.6 exponential_reduce_fusion.2
  166.1 10.3 bitcast_dynamic-update-slice_fusion.5
  176.4 9.3 multiply_reduce_fusion.8
  185.7 9.5 exponential_reduce_fusion.2
  195.2 10.2 bitcast_dynamic-update-slice_fusion.5
  220.3 48.3 %multiply_convert_fusion.3 = (bf16[1024,4096]{1,0:T(8,128)(2,1)}, f32[1024,4096]{1,0:T(8,128)}, f32[1024,4096]{1,0:T(8,128)}) fusion(f32[4096]{0:T(1024)S(1)} %bitcast.136, bf16[1024,4096]{1,0:T(8,128)(2,1)} %all-gather.10.cloned.1.call-done, bf16[1024,1024]{0,1:T(8,128)(2,1)S(1)} %fusion.59.clone.4), kind=kOutput, calls=%fused_computation.58 | convolution fusion | flops 8866758656 | bytes 52445184 | tf_op jit(solution)/shard_map/dot_general | solution.py:120
  268.6 30.5 %all-gather.12.cloned.1.call-done = bf16[4096,1024]{1,0:T(8,128)(2,1)} async-done(((bf16[128,1024]{1,0:T(8,128)(2,1)}), bf16[4096,1024]{1,0:T(8,128)(2,1)}) %all-gather.12.cloned.1.call-update) | async-done | bytes 8388624 | tf_op jit(solution)/shard_map/all_gather | solution.py:92
  299.1 14.9 %fusion.65 = (f32[1024]{0:T(1024)S(1)}, f32[1024,1024]{0,1:T(8,128)S(1)}) fusion(f32[1024]{0:T(1024)S(1)} %copy-done.40, bf16[1024,4096]{1,0:T(8,128)(2,1)} %get-tuple-element.235, bf16[4096,1024]{1,0:T(8,128)(2,1)} %all-gather.12.cloned.1.call-done, f32[1024]{0:T(1024)S(1)} %convert_element_type.103, f32[1024]{0:T(1024)S(1)} %convert_element_type.102, ...), kind=kOutput, calls=%fused_computation.119 | convolution fusion | flops 8597273600 | bytes 25190400 | tf_op jit(solution)/shard_map/dot_general | solution.py:124
  326.8 24.4 %convert_reduce_fusion = (f32[4096]{0:T(1024)}, bf16[1024,4096]{1,0:T(8,128)(2,1)}) fusion(f32[1024,4096]{1,0:T(8,128)} %get-tuple-element.236, f32[1024,4096]{1,0:T(8,128)} %get-tuple-element.249, f32[4096]{0:T(1024)S(1)} %bitcast.137, bf16[1024,1024]{0,1:T(8,128)(2,1)} %get-tuple-element.228, bf16[4096,1024]{1,0:T(8,128)(2,1)} %all-gather.12.cloned.1.call-done), kind=kOutput, calls=%fused_computation.56 | convolution fusion | flops 8661233664 | bytes 52461568 | tf_op jit(solution)/shard_map/td,fd->tf/dot_general | solution.py:140
  351.2 17.6 %multiply_reduce_fusion.2 = (f32[1024]{0:T(1024)}, f32[1024]{0:T(1024)S(1)}, f32[1024]{0:T(1024)}, f32[1024,1024]{0,1:T(8,128)S(1)}) fusion(f32[1024,1024]{0,1:T(8,128)S(1)} %copy-done.7, f32[1024]{0:T(1024)S(1)} %fusion.54, f32[1024]{0:T(1024)S(1)} %broadcast_multiply_fusion.1, f32[1024]{0:T(1024)S(1)} %convert_element_type.102, ...), kind=kOutput, calls=%fused_computation.86 | convolution fusion | flops 8607757312 | bytes 31502336 | tf_op jit(solution)/shard_map/tf,df->td/dot_general | solution.py:146
  391.8 124.6 %while.23 = (s32[]{:T(128)}, bf16[2,512,3072]{2,1,0:T(8,128)(2,1)}, bf16[2,512,16,64]{1,3,2,0:T(8,128)(2,1)}, bf16[2,512,16,64]{1,3,2,0:T(8,128)(2,1)}, f32[2,16...) while((s32[]{:T(128)}, bf16[2,512,3072]{2,1,0:T(8,128)(2,1)}, ...), condition=%wide.region_14.15_spmd, body=%wide.region_12.14_spmd.sunk | while | flops 2746736640 | bytes 268667200 | solution.py:168
  392.0 10.4 fusion.114
  402.5 8.6 fusion.115
  411.1 14.3 %multiply_reduce_fusion.9 = (f32[16,512]{1,0:T(8,128)S(1)}, f32[16,512,512]{1,2,0:T(8,128)}) fusion(f32[16,512,512]{1,2,0:T(8,128)} %fusion.114, f32[16,512]{1,0:T(8,128)S(1)} %dynamic-slice_bitcast_fusion.2, bf16[2,512,16,64]{1,3,2,0:T(8,128)(2,1)} %get-tuple-element.388, s32[]{:T(128)S(6)} %copy.139, bf16[2,512,16,64]{1,3,2,0:T(8,128)(2,1)} %copy-done.4), kind=kOutput, calls=%fused_computation.20.clone.1 | convolution fusion | flops 553639936 | bytes 35718144 | tf_op jit(solution)/shard_map/while/body/eval_jaxpr/qhd,khd->hqk/dot_general | solution.py:46
  428.2 10.6 multiply_convert_fusion.7
  454.4 10.4 fusion.114
  473.3 14.2 %multiply_reduce_fusion.9 = (f32[16,512]{1,0:T(8,128)S(1)}, f32[16,512,512]{1,2,0:T(8,128)}) fusion(f32[16,512,512]{1,2,0:T(8,128)} %fusion.114, f32[16,512]{1,0:T(8,128)S(1)} %dynamic-slice_bitcast_fusion.2, bf16[2,512,16,64]{1,3,2,0:T(8,128)(2,1)} %get-tuple-element.388, s32[]{:T(128)S(6)} %copy.139, bf16[2,512,16,64]{1,3,2,0:T(8,128)(2,1)} %copy-done.4), kind=kOutput, calls=%fused_computation.20.clone.1 | convolution fusion | flops 553639936 | bytes 35718144 | tf_op jit(solution)/shard_map/while/body/eval_jaxpr/qhd,khd->hqk/dot_general | solution.py:46
  490.5 10.6 multiply_convert_fusion.7
  516.5 12.1 %convolution_bitcast_fusion = f32[1024,3072]{0,1:T(8,128)} fusion(bf16[1024,3072]{1,0:T(8,128)(2,1)} %bitcast.132, bf16[1024,1024]{1,0:T(8,128)(2,1)} %param.19), kind=kOutput, calls=%fused_computation.73 | convolution fusion | flops 6442450944 | bytes 20971520 | tf_op jit(solution)/shard_map/td,te->de/dot_general | solution.py:170
  528.6 12.6 %copy.104 = f32[1024,3072]{1,0:T(8,128)} copy(f32[1024,3072]{0,1:T(8,128)} %convolution_bitcast_fusion) | data formatting | bytes 25165824
  541.9 16.9 %fusion.56 = f32[1024,4096]{1,0:T(8,128)} fusion(bf16[1024,4096]{1,0:T(8,128)(2,1)} %get-tuple-element.230, f32[1024,1024]{0,1:T(8,128)} %copy-done.6, f32[1024]{0:T(1024)S(1)} %copy-done.32, f32[1024]{0:T(1024)S(1)} %copy-done.23, f32[1024]{0:T(1024)S(1)} %copy-done.25, f32[1024]{0:T(1024)S(1)} %copy-done.20), kind=kOutput, calls=%fused_computation.113 | convolution fusion | flops 8595177472 | bytes 29376512 | tf_op jit(solution)/shard_map/td,tf->df/dot_general | solution.py:143
  560.5 15.1 %fusion.67 = f32[4096,1024]{1,0:T(8,128)} fusion(bf16[1024,4096]{1,0:T(8,128)(2,1)} %get-tuple-element.235, bf16[1024,1024]{0,1:T(8,128)(2,1)S(1)} %copy-done.16), kind=kOutput, calls=%fused_computation.121 | convolution fusion | flops 8589934592 | bytes 27262976 | tf_op jit(solution)/shard_map/tf,td->fd/dot_general | solution.py:138
  579.9 11.9 %add_convert_fusion.2 = bf16[1024,1024]{0,1:T(8,128)(2,1)S(1)} fusion(f32[1024,1024]{0,1:T(8,128)} %copy-done.11, f32[1024]{0:T(1024)S(1)} %copy-done.34, bf16[1024,3072]{1,0:T(8,128)(2,1)} %bitcast.133, bf16[1024,3072]{1,0:T(8,128)(2,1)} %all-gather.6.cloned.1.call-done), kind=kOutput, calls=%fused_computation.88 | convolution fusion | flops 6445596672 | bytes 18878464 | tf_op jit(solution)/shard_map/te,de->td/dot_general | solution.py:174
  600.6 42.6 %all-reduce.17 = (f32[1024]{0:T(1024)S(1)}, f32[1024]{0:T(1024)S(1)}, f32[1024]{0:T(1024)S(1)}, f32[1024]{0:T(1024)S(1)}, f32[1024]{0:T(1024)S(1)}, /*index=5*/f...) all-reduce(f32[1024]{0:T(1024)S(1)} %get-tuple-element.173, ...), channel_id=3, replica_groups=mesh['dp'=32] {'dp'}, use_global_device_ids=true, to_apply=%region_17.18.clone | all-reduce | flops 12288 | bytes 98304
  648.5 48.5 %reduce-scatter.13.cloned.1.call-done = f32[32,3072]{1,0:T(8,128)} async-done(((f32[1024,3072]{1,0:T(8,128)}), f32[32,3072]{1,0:T(8,128)}) %reduce-scatter.13.cloned.1.call-update) | async-done | bytes 393232
  697.0 184.8 %reduce-scatter.9.cloned.1.call-done = f32[32,4096]{1,0:T(8,128)} async-done(((f32[1024,4096]{1,0:T(8,128)}), f32[32,4096]{1,0:T(8,128)}) %reduce-scatter.9.cloned.1.call-update) | async-done | bytes 524304 | tf_op jit(solution)/shard_map/reduce_scatter | solution.py:150
  881.9 187.6 %reduce-scatter.11.cloned.1.call-done = f32[128,1024]{1,0:T(8,128)} async-done(((f32[4096,1024]{1,0:T(8,128)}), f32[128,1024]{1,0:T(8,128)}) %reduce-scatter.11.cloned.1.call-update) | async-done | bytes 524304 | tf_op jit(solution)/shard_map/reduce_scatter | solution.py:152
  (234 shorter events, 164.2 us)
Async XLA Ops:
  7.3 8.5 copy-start.49
  7.3 51.9 %copy-start.41 = (bf16[128]{0:T(256)(128)(2,1)S(1)}, bf16[128]{0:T(256)(128)(2,1)}, u32[]{:S(2)}) copy-start(bf16[128]{0:T(256)(128)(2,1)} %param.29) | copy-start | bytes 772
  7.3 92.2 %copy-start.13 = (bf16[1024,1024]{1,0:T(8,128)(2,1)S(1)}, bf16[1024,1024]{1,0:T(8,128)(2,1)}, u32[]{:S(2)}) copy-start(bf16[1024,1024]{1,0:T(8,128)(2,1)} %param.19) | copy-start | bytes 6291460
  7.3 96.1 %all-gather.6.cloned.1.call-start = ((), (), s32[]{:S(2)}) async-start(), calls=%async_computation.4 | async-start | bytes 6488064 | tf_op jit(solution)/shard_map/all_gather | solution.py:81
  8.0 204.0 %all-gather.8.cloned.1.call-start = ((), (), s32[]{:S(2)}) async-start(), calls=%async_computation.5 | async-start | bytes 2162688 | tf_op jit(solution)/shard_map/all_gather | solution.py:84
  8.8 211.5 %all-gather.10.cloned.1.call-start = ((), (), s32[]{:S(2)}) async-start(), calls=%async_computation.6 | async-start | bytes 8650752 | tf_op jit(solution)/shard_map/all_gather | solution.py:90
  9.5 289.6 %all-gather.12.cloned.1.call-start = ((), (), s32[]{:S(2)}) async-start(), calls=%async_computation.7 | async-start | bytes 8650752 | tf_op jit(solution)/shard_map/all_gather | solution.py:92
  10.1 638.5 %reduce-scatter.7.cloned.1.call-start = ((), (), s32[]{:S(2)}) async-start(), calls=%async_computation.8 | async-start | bytes 4325376 | tf_op jit(solution)/shard_map/reduce_scatter | solution.py:182
  102.1 197.0 %copy-start.31 = (f32[1024]{0:T(1024)}, f32[1024]{0:T(1024)S(1)}, u32[]{:S(2)}) copy-start(f32[1024]{0:T(1024)S(1)} %convert_element_type.103) | copy-start | bytes 12292
  102.1 266.7 %copy-start.22 = (f32[1024]{0:T(1024)}, f32[1024]{0:T(1024)S(1)}, u32[]{:S(2)}) copy-start(f32[1024]{0:T(1024)S(1)} %convert_element_type.102) | copy-start | bytes 12292
  217.6 151.2 %copy-start.19 = (f32[1024]{0:T(1024)}, f32[1024]{0:T(1024)S(1)}, u32[]{:S(2)}) copy-start(f32[1024]{0:T(1024)S(1)} %broadcast_multiply_fusion.1) | copy-start | bytes 12292
  218.1 50.5 %copy-start.26 = (f32[1024]{0:T(1024)}, f32[1024]{0:T(1024)S(1)}, u32[]{:S(2)}) copy-start(f32[1024]{0:T(1024)S(1)} %multiply_reduce_fusion.5) | copy-start | bytes 12292
  219.5 149.3 %copy-start.24 = (f32[1024]{0:T(1024)}, f32[1024]{0:T(1024)S(1)}, u32[]{:S(2)}) copy-start(f32[1024]{0:T(1024)S(1)} %fusion.54) | copy-start | bytes 12292
  220.3 78.8 %copy-start.40 = (f32[1024]{0:T(1024)S(1)}, f32[1024]{0:T(1024)}, u32[]{:S(2)}) copy-start(f32[1024]{0:T(1024)} %convert_element_type.107) | copy-start | bytes 12292
  299.1 15.0 %copy-start.21 = (f32[1024]{0:T(1024)S(1)}, f32[1024]{0:T(1024)}, u32[]{:S(2)}) copy-start(f32[1024]{0:T(1024)} %convert_element_type.108) | copy-start | bytes 12292
  314.0 8.6 copy-start.8
  326.8 24.4 %copy-start.7 = (f32[1024,1024]{0,1:T(8,128)S(1)}, f32[1024,1024]{0,1:T(8,128)}, u32[]{:S(2)}) copy-start(f32[1024,1024]{0,1:T(8,128)} %copy-done.6) | copy-start | bytes 12582916
  326.8 24.4 %copy-start.10 = (bf16[1024,1024]{0,1:T(8,128)(2,1)S(1)}, bf16[1024,1024]{0,1:T(8,128)(2,1)}, u32[]{:S(2)}) copy-start(bf16[1024,1024]{0,1:T(8,128)(2,1)} %copy.84) | copy-start | bytes 6291460
  351.2 17.6 %copy-start.27 = (f32[1024]{0:T(1024)S(1)}, f32[1024]{0:T(1024)}, u32[]{:S(2)}) copy-start(f32[1024]{0:T(1024)} %copy-done.26) | copy-start | bytes 12292
  391.8 305.2 %reduce-scatter.13.cloned.1.call-start = ((), (), s32[]{:S(2)}) async-start(), calls=%async_computation.11 | async-start | bytes 12976128
  392.0 10.5 copy-start.4
  411.0 14.3 %slice-start = ((s8[16777216]{0:T(1024)(128)(4,1)}), s8[4194304]{0:T(1024)(128)(4,1)S(1)}, s32[]{:S(2)}) async-start(s8[16777216]{0:T(1024)(128)(4,1)} %bitcast.126), calls=%async_computation.12 | async-start | bytes 8388608 | tf_op jit(solution)/shard_map/while
  411.1 14.3 %slice-start.1 = ((s8[16777216]{0:T(1024)(128)(4,1)}), s8[4194304]{0:T(1024)(128)(4,1)S(1)}, s32[]{:S(2)}) async-start(s8[16777216]{0:T(1024)(128)(4,1)} %bitcast.126), calls=%async_computation.13 | async-start | bytes 8388608 | tf_op jit(solution)/shard_map/while
  411.1 16.0 %slice-start.2 = ((s8[16777216]{0:T(1024)(128)(4,1)}), s8[4194304]{0:T(1024)(128)(4,1)S(1)}, s32[]{:S(2)}) async-start(s8[16777216]{0:T(1024)(128)(4,1)} %bitcast.126), calls=%async_computation.14 | async-start | bytes 8388608 | tf_op jit(solution)/shard_map/while
  411.1 17.2 %slice-start.3 = ((s8[16777216]{0:T(1024)(128)(4,1)}), s8[4194304]{0:T(1024)(128)(4,1)S(1)}, s32[]{:S(2)}) async-start(s8[16777216]{0:T(1024)(128)(4,1)} %bitcast.126), calls=%async_computation.15 | async-start | bytes 8388608 | tf_op jit(solution)/shard_map/while
  454.4 10.5 copy-start.4
  473.3 14.2 %slice-start = ((s8[16777216]{0:T(1024)(128)(4,1)}), s8[4194304]{0:T(1024)(128)(4,1)S(1)}, s32[]{:S(2)}) async-start(s8[16777216]{0:T(1024)(128)(4,1)} %bitcast.126), calls=%async_computation.12 | async-start | bytes 8388608 | tf_op jit(solution)/shard_map/while
  473.3 14.2 %slice-start.1 = ((s8[16777216]{0:T(1024)(128)(4,1)}), s8[4194304]{0:T(1024)(128)(4,1)S(1)}, s32[]{:S(2)}) async-start(s8[16777216]{0:T(1024)(128)(4,1)} %bitcast.126), calls=%async_computation.13 | async-start | bytes 8388608 | tf_op jit(solution)/shard_map/while
  473.3 15.9 %slice-start.2 = ((s8[16777216]{0:T(1024)(128)(4,1)}), s8[4194304]{0:T(1024)(128)(4,1)S(1)}, s32[]{:S(2)}) async-start(s8[16777216]{0:T(1024)(128)(4,1)} %bitcast.126), calls=%async_computation.14 | async-start | bytes 8388608 | tf_op jit(solution)/shard_map/while
  473.3 17.1 %slice-start.3 = ((s8[16777216]{0:T(1024)(128)(4,1)}), s8[4194304]{0:T(1024)(128)(4,1)S(1)}, s32[]{:S(2)}) async-start(s8[16777216]{0:T(1024)(128)(4,1)} %bitcast.126), calls=%async_computation.15 | async-start | bytes 8388608 | tf_op jit(solution)/shard_map/while
  541.2 340.6 %reduce-scatter.9.cloned.1.call-start = ((), (), s32[]{:S(2)}) async-start(), calls=%async_computation.9 | async-start | bytes 17301504 | tf_op jit(solution)/shard_map/reduce_scatter | solution.py:150
  558.8 510.6 %reduce-scatter.11.cloned.1.call-start = ((), (), s32[]{:S(2)}) async-start(), calls=%async_computation.10 | async-start | bytes 17301504 | tf_op jit(solution)/shard_map/reduce_scatter | solution.py:152
  (39 other events, 144.8 us)
Sparse Core Ops, SparseCore 0:
  11.0 72.1 all-gather.5
  86.1 54.8 all-gather.7
  143.9 76.3 all-gather.9
  223.0 76.0 all-gather.11
  391.9 139.5 reduce-scatter.6
  541.3 155.6 reduce-scatter.12
  700.0 181.8 reduce-scatter.8
  884.8 184.5 reduce-scatter.10
where the time goes:
time: 1080 us
  waiting for transfers between devices  454 us (42%)
  matrix products  307 us (28%)
  blocking collectives  126 us (12%)
  local copies, waits for them, and re-layouts  111 us (10%)
  other arithmetic  63.5 us (6%)
  between operations  14.9 us (1%)
    reduce_scatter x1, waiting for transfers between devices, local(): lax.psum_scatter(mlp_terms[2], 'dp', scatter_dimension=0, tiled=True)  188 us
    reduce_scatter x1, waiting for transfers between devices, local(): lax.psum_scatter(mlp_terms[0], 'dp', scatter_dimension=0, tiled=True)  185 us
    unnamed x2, blocking collectives  85.2 us
    unnamed x9, waiting for transfers between devices  51.1 us
    dot_general x1, matrix products, local(): jnp.dot(normed_low, full_up, preferred_element_type=jnp.float32)  48.3 us
    unnamed x122, local copies, waits for them, and re-layouts  42.4 us
    all_gather x1, blocking collectives, local(): lax.all_gather(up_bias, 'dp', axis=0, tiled=True)  40.3 us
    all_gather x1, waiting for transfers between devices, local(): lax.all_gather(w_down, 'dp', axis=0, tiled=True)  30.5 us
  transfers between devices with their start and end apart: 8, of which 5 were waited for; matrix products, arithmetic and copies ran while one was open for 35% of the time, Pallas kernels for 0%

commit v1 on v0

v1 whole, which is shorter than its diff:
```python
import functools
import math

import jax
import jax.numpy as jnp
from jax import lax
from jax.experimental import pallas as pl
from jax.experimental.pallas import tpu as pltpu
from jax.sharding import PartitionSpec as P

HD = 64
LEN = 512
EPS = 1e-05
CHUNKS = 32
F32 = jnp.float32
BF16 = jnp.bfloat16
MIB = 1 << 20


def params(limit=48):
    return pltpu.CompilerParams(vmem_limit_bytes=limit * MIB)


COST = 0.02


def cost(flops, nbytes, trans=0):
    return pl.CostEstimate(
        flops=int(COST * flops), bytes_accessed=int(COST * nbytes), transcendentals=int(COST * trans)
    )


def dot(a, b):
    return jnp.dot(a, b, preferred_element_type=F32)


def dot_t(a, b):
    return lax.dot_general(a, b, (((1,), (1,)), ((), ())), preferred_element_type=F32)


def t_dot(a, b):
    return lax.dot_general(a, b, (((0,), (0,)), ((), ())), preferred_element_type=F32)


SCALAR = pl.BlockSpec(memory_space=pltpu.SMEM)


def row_spec(block, width):
    return pl.BlockSpec((block, width), lambda i: (i, 0))


def full_spec(shape):
    return pl.BlockSpec(shape, lambda i: (0,) * len(shape))


def project_kernel(me_ref, x_ref, *refs):
    pieces, (o_ref, w_ref, t_ref, sems) = refs[:4], refs[4:]
    j = pl.program_id(0)
    block = o_ref.shape[1]
    width = x_ref.shape[1]
    size = width // CHUNKS

    @pl.when(j == 0)
    def _():
        cut = pieces[0].shape[2]
        copies = []
        for which, piece in enumerate(pieces):
            right, core = which % 2, which // 2
            for k in range(piece.shape[0]):
                a, b, z = k >> 3, (k >> 2) & 1, k & 3
                mask = core | (a << 1 | b << 2 if right else a << 2 | b << 1) | z << 3
                at = pl.multiple_of(jnp.bitwise_xor(me_ref[0], mask) * size, size)
                cols = pl.ds(cut, piece.shape[2]) if right else pl.ds(0, cut)
                copies.append(
                    pltpu.make_async_copy(
                        piece.at[k], w_ref.at[pl.ds(at, size), cols], sems.at[len(copies)]
                    )
                )
        for copy in copies:
            copy.start()
        for copy in copies:
            copy.wait()
        table = w_ref[:, 3 * width :].astype(F32).T
        t_ref[...] = table[: t_ref.shape[0]]

    per = width // block
    at = pl.multiple_of((j % per) * block, block)
    bias = jnp.where(
        j < per,
        t_ref[0:1, pl.ds(at, block)],
        jnp.where(j >= 2 * per, t_ref[1:2, pl.ds(at, block)], 0.0),
    )
    w = w_ref[:, pl.ds(pl.multiple_of(j * block, block), block)]
    o_ref[...] = (dot(x_ref[...], w) + bias).astype(BF16)


def project(me, x, pieces, block=512):
    rows, width = x.shape
    cols = 3 * width
    held = pieces[0].shape[2] + pieces[1].shape[2]
    return pl.pallas_call(
        project_kernel,
        grid=(cols // block,),
        in_specs=[SCALAR, full_spec((rows, width))] + [pl.BlockSpec(memory_space=pl.ANY)] * 4,
        out_specs=[
            pl.BlockSpec((rows, block), lambda j: (0, j)),
            full_spec((width, held)),
            full_spec((16, width)),
        ],
        out_shape=[
            jax.ShapeDtypeStruct((rows, cols), BF16),
            jax.ShapeDtypeStruct((width, held), BF16),
            jax.ShapeDtypeStruct((16, width), F32),
        ],
        scratch_shapes=[pltpu.SemaphoreType.DMA((2 * CHUNKS,))],
        compiler_params=params(),
        cost_estimate=cost(2 * rows * width * cols, 2 * (rows * width + 2 * width * cols + rows * cols)),
        name="project",
    )(me, x, *pieces)


def head_mask(shape, h):
    lane = lax.broadcasted_iota(jnp.int32, shape, 1)
    return (lane >= h * HD) & (lane < (h + 1) * HD)


def attend_kernel(q_ref, k_ref, v_ref, ctx_ref, lse_ref):
    q = q_ref[...] * jnp.asarray(1.0 / math.sqrt(HD), BF16)
    k = k_ref[...]
    vt = v_ref[...].T
    parts = []
    for h in range(2):
        qh = jnp.where(head_mask(q.shape, h), q, jnp.zeros_like(q))
        s = dot_t(k, qh)
        m = jnp.max(s, axis=0, keepdims=True)
        e = jnp.exp(s - m)
        total = jnp.sum(e, axis=0, keepdims=True)
        c = dot(vt[h * HD : (h + 1) * HD, :], e.astype(BF16))
        parts.append(c * (1.0 / total))
        lse_ref[0, 0, h : h + 1, :] = m + jnp.log(total)
    ctx_ref[...] = jnp.concatenate(parts, axis=0).T.astype(BF16)


def attend(qkv, width):
    rows = qkv.shape[0]
    count, pairs = rows // LEN, width // 128
    return pl.pallas_call(
        attend_kernel,
        grid=(pairs, count),
        in_specs=[
            pl.BlockSpec((LEN, 128), lambda p, s: (s, p)),
            pl.BlockSpec((LEN, 128), lambda p, s: (s, pairs + p)),
            pl.BlockSpec((LEN, 128), lambda p, s: (s, 2 * pairs + p)),
        ],
        out_specs=[
            pl.BlockSpec((LEN, 128), lambda p, s: (s, p)),
            pl.BlockSpec((1, 1, 2, LEN), lambda p, s: (p, s, 0, 0)),
        ],
        out_shape=[
            jax.ShapeDtypeStruct((rows, width), BF16),
            jax.ShapeDtypeStruct((pairs, count, 2, LEN), F32),
        ],
        compiler_params=params(),
        cost_estimate=cost(
            rows * width * LEN * 4 * 4, 8 * rows * width, rows * width * LEN // HD
        ),
        name="attend",
    )(qkv, qkv, qkv)


def attend_back_kernel(q_ref, k_ref, v_ref, c_ref, d_ref, lse_ref, dp_ref, sq_ref, sv_ref):
    scale = 1.0 / math.sqrt(HD)
    q = q_ref[...] * jnp.asarray(scale, BF16)
    k = k_ref[...]
    v = v_ref[...]
    d = d_ref[...]
    kt = k.T
    prod = (d.astype(F32) * c_ref[...].astype(F32)).T
    dk = dv = None
    parts = []
    for h in range(2):
        mask = head_mask(q.shape, h)
        qh = jnp.where(mask, q, jnp.zeros_like(q))
        dh = jnp.where(mask, d, jnp.zeros_like(d))
        delta = jnp.sum(prod[h * HD : (h + 1) * HD, :], axis=0, keepdims=True)
        p = jnp.exp(dot_t(k, qh) - lse_ref[0, 0, h : h + 1, :])
        ds = (p * (dot_t(v, dh) - delta)).astype(BF16)
        dv_h = dot(p.astype(BF16), dh)
        dk_h = dot(ds, qh)
        dv = dv_h if dv is None else dv + dv_h
        dk = dk_h if dk is None else dk + dk_h
        parts.append(dot(kt[h * HD : (h + 1) * HD, :], ds) * scale)
    dq = jnp.concatenate(parts, axis=0).T.astype(BF16)
    dv = dv.astype(BF16)
    dp_ref[:, 0:128] = dq
    dp_ref[:, 128:256] = dk.astype(BF16)
    dp_ref[:, 256:384] = dv
    sq = jnp.sum(dq.astype(F32), axis=0, keepdims=True)
    sv = jnp.sum(dv.astype(F32), axis=0, keepdims=True)
    first = pl.program_id(1) == 0

    @pl.when(first)
    def _():
        sq_ref[...] = sq
        sv_ref[...] = sv

    @pl.when(jnp.logical_not(first))
    def _():
        sq_ref[...] += sq
        sv_ref[...] += sv


def attend_back(qkv, ctx, dctx, lse, width, start, n_pairs):
    rows = qkv.shape[0]
    count, pairs = rows // LEN, width // 128
    cols = n_pairs * 128
    sum_block = pl.BlockSpec((1, 128), lambda p, s: (0, p))
    return pl.pallas_call(
        attend_back_kernel,
        grid=(n_pairs, count),
        in_specs=[
            pl.BlockSpec((LEN, 128), lambda p, s: (s, start + p)),
            pl.BlockSpec((LEN, 128), lambda p, s: (s, pairs + start + p)),
            pl.BlockSpec((LEN, 128), lambda p, s: (s, 2 * pairs + start + p)),
            pl.BlockSpec((LEN, 128), lambda p, s: (s, start + p)),
            pl.BlockSpec((LEN, 128), lambda p, s: (s, start + p)),
            pl.BlockSpec((1, 1, 2, LEN), lambda p, s: (start + p, s, 0, 0)),
        ],
        out_specs=[pl.BlockSpec((LEN, 384), lambda p, s: (s, p)), sum_block, sum_block],
        out_shape=[jax.ShapeDtypeStruct((rows, 3 * cols), BF16)]
        + [jax.ShapeDtypeStruct((1, cols), F32)] * 2,
        compiler_params=params(),
        cost_estimate=cost(rows * cols * LEN * 10 * 4, 16 * rows * cols, rows * cols * LEN // HD),
        name="attend_back",
    )(qkv, qkv, qkv, ctx, dctx, lse)


def out_weight(held):
    _, rows, width = held.shape
    size = width // CHUNKS
    return pl.BlockSpec((CHUNKS, size, width), lambda i: (0, rows // size - 1, 0))


def deep_weight(held, which):
    _, rows, width = held.shape
    return pl.BlockSpec((CHUNKS, (rows - width // CHUNKS) // 2, width), lambda i: (0, which, 0))


def out_norm_kernel(c_ref, w_ref, b_ref, x_ref, g_ref, s_ref, hat_ref, rstd_ref, low_ref):
    w = w_ref[...].reshape(-1, x_ref.shape[1])
    h = x_ref[...].astype(F32) + (dot(c_ref[...], w) + b_ref[...])
    center = h - jnp.mean(h, axis=-1, keepdims=True)
    rstd = lax.rsqrt(jnp.mean(center * center, axis=-1, keepdims=True) + EPS)
    hat = center * rstd
    hat_ref[...] = hat
    rstd_ref[...] = rstd
    low_ref[...] = (hat * g_ref[...] + s_ref[...]).astype(BF16)


def out_norm(ctx, held, bias, tokens, gain, shift, block=256):
    rows, width = tokens.shape
    vec = full_spec((1, width))
    return pl.pallas_call(
        out_norm_kernel,
        grid=(rows // block,),
        in_specs=[
            row_spec(block, width),
            out_weight(held),
            vec,
            row_spec(block, width),
            vec,
            vec,
        ],
        out_specs=[row_spec(block, width), row_spec(block, 1), row_spec(block, width)],
        out_shape=[
            jax.ShapeDtypeStruct((rows, width), F32),
            jax.ShapeDtypeStruct((rows, 1), F32),
            jax.ShapeDtypeStruct((rows, width), BF16),
        ],
        compiler_params=params(),
        cost_estimate=cost(2 * rows * width * width, 14 * rows * width),
        name="out_norm",
    )(ctx, held, bias, tokens, gain, shift)


ERF_P = 0.3275911 / math.sqrt(2.0)
ERF_A = (0.254829592, -0.284496736, 1.421413741, -1.453152027, 1.061405429)


def gelu_pair(u):
    t = 1.0 / (1.0 + ERF_P * jnp.abs(u))
    e = jnp.exp(-0.5 * (u * u))
    poly = t * (ERF_A[0] + t * (ERF_A[1] + t * (ERF_A[2] + t * (ERF_A[3] + t * ERF_A[4]))))
    tail = 0.5 * poly * e
    cdf = jnp.where(u >= 0, 1.0 - tail, tail)
    return u * cdf, cdf + u * e * (1.0 / math.sqrt(2.0 * math.pi))


def up_kernel(x_ref, w_ref, b_ref, act_ref, slope_ref):
    block = act_ref.shape[1]
    u = dot(x_ref[...], w_ref[...].reshape(-1, block)) + b_ref[...]
    act, slope = gelu_pair(u)
    act_ref[...] = act.astype(BF16)
    slope_ref[...] = slope.astype(BF16)


def up_gelu(x, held, bias, block=512):
    rows, width = x.shape
    cols = bias.shape[1]
    per = width // block
    col = pl.BlockSpec((rows, block), lambda j: (0, j))
    return pl.pallas_call(
        up_kernel,
        grid=(cols // block,),
        in_specs=[
            full_spec((rows, width)),
            pl.BlockSpec((CHUNKS, width // CHUNKS, block), lambda j: (0, j // per, j % per)),
            pl.BlockSpec((1, block), lambda j: (0, j)),
        ],
        out_specs=[col, col],
        out_shape=[jax.ShapeDtypeStruct((rows, cols), BF16)] * 2,
        compiler_params=params(),
        cost_estimate=cost(
            2 * rows * width * cols, 2 * (width * cols + 2 * rows * cols), 2 * rows * cols
        ),
        name="up_gelu",
    )(x, held, bias)


def down_norm_kernel(
    a_ref, w_ref, b_ref, hat1_ref, g1_ref, s1_ref, g2_ref, s2_ref, cot_ref,
    out_ref, dh_ref, dm_ref, dg_ref, ds_ref, db_ref,
):
    n1 = hat1_ref[...] * g1_ref[...] + s1_ref[...]
    h = n1 + (dot(a_ref[...], w_ref[...].reshape(-1, n1.shape[1])) + b_ref[...])
    center = h - jnp.mean(h, axis=-1, keepdims=True)
    rstd = lax.rsqrt(jnp.mean(center * center, axis=-1, keepdims=True) + EPS)
    hat = center * rstd
    out_ref[...] = (hat * g2_ref[...] + s2_ref[...]).astype(BF16)
    cot = cot_ref[...].astype(F32)
    wide = cot * g2_ref[...]
    mean_a = jnp.mean(wide, axis=-1, keepdims=True)
    mean_b = jnp.mean(wide * hat, axis=-1, keepdims=True)
    dh = rstd * (wide - mean_a - hat * mean_b)
    dh_ref[...] = dh
    dm = dh.astype(BF16)
    dm_ref[...] = dm

    @pl.when(pl.program_id(0) == 0)
    def _():
        dg_ref[...] = jnp.zeros_like(dg_ref)
        ds_ref[...] = jnp.zeros_like(ds_ref)
        db_ref[...] = jnp.zeros_like(db_ref)

    dg_ref[...] += jnp.sum(cot * hat, axis=0, keepdims=True)
    ds_ref[...] += jnp.sum(cot, axis=0, keepdims=True)
    db_ref[...] += jnp.sum(dm.astype(F32), axis=0, keepdims=True)


def down_norm(act, held, bias, hat1, g1, s1, g2, s2, cot, block=256):
    rows, width = hat1.shape
    deep = act.shape[1]
    vec = full_spec((1, width))
    row = row_spec(block, width)
    return pl.pallas_call(
        down_norm_kernel,
        grid=(rows // block,),
        in_specs=[row_spec(block, deep), deep_weight(held, 1), vec, row, vec, vec, vec, vec, row],
        out_specs=[row, row, row, vec, vec, vec],
        out_shape=[
            jax.ShapeDtypeStruct((rows, width), BF16),
            jax.ShapeDtypeStruct((rows, width), F32),
            jax.ShapeDtypeStruct((rows, width), BF16),
        ]
        + [jax.ShapeDtypeStruct((1, width), F32)] * 3,
        compiler_params=params(),
        cost_estimate=cost(2 * rows * width * deep, 2 * deep * (rows + width) + 14 * rows * width),
        name="down_norm",
    )(act, held, bias, hat1, g1, s1, g2, s2, cot)


def split(value, core, chunk, keep_ref, send_ref):
    value = value.astype(BF16).reshape(-1, 2, 2, chunk // 2, value.shape[1])
    for half in range(2):
        even = value[:, 0, half].reshape(keep_ref.shape[1:])
        odd = value[:, 1, half].reshape(keep_ref.shape[1:])
        keep_ref[half] = jnp.where(core == 0, even, odd)
        send_ref[half] = jnp.where(core == 0, odd, even)


def join(keep, send, chunk):
    cols = keep.shape[-1]
    pair = [v.reshape(2, -1, chunk // 2, cols) for v in (keep, send)]
    return jnp.stack(pair, axis=0).transpose(2, 0, 1, 3, 4).reshape(-1, cols)


def down_grad_kernel(core_ref, a_ref, b_ref, keep_ref, send_ref):
    chunk = keep_ref.shape[1]
    split(t_dot(a_ref[...], b_ref[...]), core_ref[0], chunk, keep_ref, send_ref)


def down_grad(core, a, b):
    rows, deep = a.shape
    cols = b.shape[1]
    block = 4 * deep // CHUNKS
    out = pl.BlockSpec((2, block // 4, cols), lambda j: (0, j, 0))
    return pl.pallas_call(
        down_grad_kernel,
        grid=(deep // block,),
        in_specs=[SCALAR, pl.BlockSpec((rows, block), lambda j: (0, j)), full_spec((rows, cols))],
        out_specs=[out, out],
        out_shape=[jax.ShapeDtypeStruct((2, deep // 4, cols), BF16)] * 2,
        compiler_params=params(),
        cost_estimate=cost(2 * rows * deep * cols, 2 * (rows * deep + rows * cols + deep * cols)),
        name="down_grad",
    )(core, a, b)


def attn_grad_kernel(core_ref, xt_ref, *refs, n_parts, more):
    parts, rest = refs[:n_parts], refs[n_parts:]
    keep_ref, send_ref = rest[-2:]
    chunk = 32
    at = 0

    def put(value):
        nonlocal at
        cols = value.shape[1]
        here = [ref.at[:, :, at : at + cols] for ref in (keep_ref, send_ref)]
        split(value, core_ref[0], chunk, *here)
        at += cols

    for ref in parts:
        put(dot(xt_ref[...], ref[...]))
    if more == "out":
        put(t_dot(rest[0][...], rest[1][...]))
    else:
        put(rest[0][...])


def attn_grad(core, xt, parts, extra, more, block=256):
    width, rows = xt.shape
    in_specs = [SCALAR, row_spec(block, rows)] + [full_spec(p.shape) for p in parts]
    cols = sum(p.shape[1] for p in parts)
    if more == "out":
        in_specs += [pl.BlockSpec((rows, block), lambda i: (0, i)), full_spec(extra[1].shape)]
        cols += extra[1].shape[1]
    else:
        in_specs += [row_spec(block, extra[0].shape[1])]
        cols += extra[0].shape[1]
    out = pl.BlockSpec((2, block // 4, cols), lambda i: (0, i, 0))
    return pl.pallas_call(
        functools.partial(attn_grad_kernel, n_parts=len(parts), more=more),
        grid=(width // block,),
        in_specs=in_specs,
        out_specs=[out, out],
        out_shape=[jax.ShapeDtypeStruct((2, width // 4, cols), BF16)] * 2,
        compiler_params=params(),
        cost_estimate=cost(2 * rows * width * cols, 2 * (rows * width + cols * (rows + width))),
        name="attn_grad",
    )(core, xt, *parts, *extra)


def up_back_kernel(
    core_ref, dm_ref, w_ref, slope_ref, x_ref, du_ref, keep_ref, send_ref, db_ref, xt_ref
):
    @pl.when(pl.program_id(0) == 0)
    def _():
        xt_ref[...] = x_ref[...].T

    w = w_ref[...].reshape(-1, dm_ref.shape[1])
    du = (dot_t(dm_ref[...], w) * slope_ref[...].astype(F32)).astype(BF16)
    du_ref[...] = du
    db_ref[...] = jnp.sum(du.astype(F32), axis=0, keepdims=True)
    split(dot(xt_ref[...], du), core_ref[0], xt_ref.shape[0] // CHUNKS, keep_ref, send_ref)


def up_back(core, dm, held, slope, x):
    rows, width = dm.shape
    deep = slope.shape[1]
    block = 4 * deep // CHUNKS
    col = pl.BlockSpec((rows, block), lambda j: (0, j))
    half = pl.BlockSpec((2, width // 4, block), lambda j: (0, 0, j))
    return pl.pallas_call(
        up_back_kernel,
        grid=(deep // block,),
        in_specs=[
            SCALAR,
            full_spec((rows, width)),
            pl.BlockSpec((4, deep // CHUNKS, width), lambda j: (j, 1, 0)),
            col,
            full_spec((rows, width)),
        ],
        out_specs=[col, half, half, pl.BlockSpec((1, block), lambda j: (0, j))],
        out_shape=[
            jax.ShapeDtypeStruct((rows, deep), BF16),
            jax.ShapeDtypeStruct((2, width // 4, deep), BF16),
            jax.ShapeDtypeStruct((2, width // 4, deep), BF16),
            jax.ShapeDtypeStruct((1, deep), F32),
        ],
        scratch_shapes=[pltpu.VMEM((width, rows), BF16)],
        compiler_params=params(),
        cost_estimate=cost(4 * rows * width * deep, 4 * deep * (rows + width) + 4 * rows * width),
        name="up_back",
    )(core, dm, held, slope, x)


def norm_back_kernel(
    du_ref, w_ref, dh2_ref, hat_ref, rstd_ref, g_ref, dh_ref, da_ref, dg_ref, ds_ref, db_ref
):
    width = dh2_ref.shape[1]
    dn = dh2_ref[...]
    size = width // CHUNKS
    for j in range(du_ref.shape[1] // width):
        w = w_ref[:, j * size : (j + 1) * size, :].reshape(width, width)
        dn = dn + dot_t(du_ref[:, j * width : (j + 1) * width], w)
    hat = hat_ref[...]
    wide = dn * g_ref[...]
    mean_a = jnp.mean(wide, axis=-1, keepdims=True)
    mean_b = jnp.mean(wide * hat, axis=-1, keepdims=True)
    dh = rstd_ref[...] * (wide - mean_a - hat * mean_b)
    dh_ref[...] = dh
    da = dh.astype(BF16)
    da_ref[...] = da

    @pl.when(pl.program_id(0) == 0)
    def _():
        dg_ref[...] = jnp.zeros_like(dg_ref)
        ds_ref[...] = jnp.zeros_like(ds_ref)
        db_ref[...] = jnp.zeros_like(db_ref)

    dg_ref[...] += jnp.sum(dn * hat, axis=0, keepdims=True)
    ds_ref[...] += jnp.sum(dn, axis=0, keepdims=True)
    db_ref[...] += jnp.sum(da.astype(F32), axis=0, keepdims=True)


def norm_back(du, held, dh2, hat, rstd, gain, block=256):
    rows, width = hat.shape
    deep = du.shape[1]
    vec = full_spec((1, width))
    row = row_spec(block, width)
    return pl.pallas_call(
        norm_back_kernel,
        grid=(rows // block,),
        in_specs=[row_spec(block, deep), deep_weight(held, 0), row, row, row_spec(block, 1), vec],
        out_specs=[row, row, vec, vec, vec],
        out_shape=[
            jax.ShapeDtypeStruct((rows, width), F32),
            jax.ShapeDtypeStruct((rows, width), BF16),
        ]
        + [jax.ShapeDtypeStruct((1, width), F32)] * 3,
        compiler_params=params(),
        cost_estimate=cost(2 * rows * width * deep, 2 * deep * (rows + width) + 14 * rows * width),
        name="norm_back",
    )(du, held, dh2, hat, rstd, gain)


def context_back_kernel(da_ref, w_ref, o_ref):
    o_ref[...] = dot_t(da_ref[...], w_ref[...].reshape(-1, da_ref.shape[1])).astype(BF16)


def context_back(da, held, block=512):
    rows, width = da.shape
    return pl.pallas_call(
        context_back_kernel,
        grid=(rows // block,),
        in_specs=[row_spec(block, width), out_weight(held)],
        out_specs=row_spec(block, width),
        out_shape=jax.ShapeDtypeStruct((rows, width), BF16),
        compiler_params=params(),
        cost_estimate=cost(2 * rows * width * width, 6 * rows * width),
        name="context_back",
    )(da, held)


def input_back_kernel(*refs):
    *parts, w_ref, dh_ref, o_ref = refs
    width = o_ref.shape[1]
    total = dh_ref[...]
    for which in range(3):
        pieces = [
            ref[:, at : at + 128]
            for ref in parts
            for at in range(which * 128, ref.shape[1], 384)
        ]
        col = which * width
        total = total + dot_t(jnp.concatenate(pieces, axis=1), w_ref[:, col : col + width])
    o_ref[...] = total.astype(BF16)


def input_back(parts, w, dh, block=256):
    rows, width = dh.shape
    return pl.pallas_call(
        input_back_kernel,
        grid=(rows // block,),
        in_specs=[row_spec(block, p.shape[1]) for p in parts]
        + [pl.BlockSpec((width, 3 * width), lambda i: (0, 0)), row_spec(block, width)],
        out_specs=row_spec(block, width),
        out_shape=jax.ShapeDtypeStruct((rows, width), BF16),
        compiler_params=params(),
        cost_estimate=cost(6 * rows * width * width, 18 * rows * width),
        name="input_back",
    )(*parts, w, dh)


def exchange(x, n, mask):
    return lax.ppermute(x, "dp", [(i, i ^ mask) for i in range(n)])


def pick(x, axis, index):
    return lax.dynamic_index_in_dim(x, index, axis, keepdims=False)


def tie(*values):
    return lax.optimization_barrier(values)


class Scatter:
    def __init__(self, keep, send, n, r):
        self.n, self.h, self.me, self.cols = n, r // 2, lax.axis_index("dp"), keep.shape[-1]
        self.held = [(keep, exchange(send, n, 1))] * 2
        self.left = [[4, 3, 2, 1], [4, 3, 2, 1]]
        self.step = 0

    def part(self, side, bit, which):
        left = self.left[side]
        at, size = left.index(bit), 1 << len(left)
        shape = (1 << at, 2, size >> (at + 1), self.h, self.cols)
        total = None
        for value in self.held[side]:
            lead = value.size // math.prod(shape)
            value = value.reshape(lead, *shape)
            start = (side if lead == 2 else 0, 0, which, 0, 0, 0)
            value = lax.dynamic_slice(value, start, (1, shape[0], 1, *shape[2:])).astype(F32)
            total = value if total is None else total + value
        return total.reshape(size // 2, self.h, self.cols)

    def behind(self, along):
        pairs = list(self.held)
        flat = tie(*pairs[0], *pairs[1], *along)
        self.held = [flat[:2], flat[2:4]]
        return flat[4:]

    def halve(self, *along):
        along = self.behind(along)
        bits = ((2, 1), (1, 2))
        sums = []
        for side in range(2):
            bit = bits[side][self.step]
            mine = (self.me >> bit) & 1
            sums += [self.part(side, bit, which).astype(BF16) for which in (1 - mine, mine)]
        *sums, = tie(*sums, *along)
        sums, along = sums[:4], sums[4:]
        for side in range(2):
            bit = bits[side][self.step]
            self.held[side] = (sums[2 * side + 1], exchange(sums[2 * side], self.n, 1 << bit))
            self.left[side].remove(bit)
        self.step += 1
        return along[0] if len(along) == 1 else along

    def column_one(self, *along):
        along = self.behind(along)
        mine = self.me >> 4
        sent, kept = [
            jnp.concatenate([self.part(side, 4, which) for side in range(2)], axis=1).astype(BF16)
            for which in (1 - mine, mine)
        ]
        sent, kept, *along = tie(sent, kept, *along)
        self.pair = (kept, exchange(sent, self.n, 16))
        return along[0] if len(along) == 1 else along

    def column_two(self, *along):
        *self.pair, = tie(*self.pair, *along)
        self.pair, along = self.pair[:2], self.pair[2:]
        mine = (self.me >> 3) & 1
        sent, kept = [
            sum(pick(value, 0, which).astype(F32) for value in self.pair) for which in (1 - mine, mine)
        ]
        sent, kept, *along = tie(sent.astype(BF16), kept, *along)
        self.last = [kept, exchange(sent, self.n, 8)]
        return along[0] if len(along) == 1 else along

    def column(self, *along):
        along = self.behind(along)
        mine = self.me >> 3
        sums = [
            jnp.concatenate(
                [
                    sum(pick(v, 0, mine ^ k).astype(F32) for v in self.held[side])
                    for side in range(2)
                ],
                axis=0,
            )
            for k in range(4)
        ]
        *sums, = tie(sums[0], *[v.astype(BF16) for v in sums[1:]], *along)
        sums, along = sums[:4], sums[4:]
        self.last = sums[:1] + [exchange(sums[k], self.n, k << 3) for k in (1, 2, 3)]
        return along[0] if len(along) == 1 else along

    def result(self):
        return sum(value.astype(F32) for value in self.last)


class PlainScatter:
    def __init__(self, keep, send, n, r):
        whole = join(keep, send, keep.shape[1] * 4 // CHUNKS)
        self.total = lax.psum_scatter(whole.astype(F32), "dp", scatter_dimension=0, tiled=True)

    def halve(self, *along):
        return along[0] if len(along) == 1 else along

    column = column_one = column_two = halve

    def result(self):
        return self.total


def gather(x):
    return lax.all_gather(x, "dp", axis=0, tiled=True)


def gather_pieces(x, n):
    cut = x.shape[1] // 256 * 128
    near = [x] + [exchange(x, n, k << 3) for k in (1, 2, 3)]
    sides = []
    for low, high, bits in ((0, cut, (1, 2)), (cut, x.shape[1], (2, 1))):
        side = jnp.concatenate([v[:, low:high] for v in near], axis=0)
        sides.append((side, bits))
    for step in range(2):
        sides = [
            (jnp.concatenate([v, exchange(v, n, 1 << bits[step])], axis=0), bits) for v, bits in sides
        ]
    mine = [v for v, _ in sides]
    pieces = mine + [exchange(v, n, 1) for v in mine]
    return [v.reshape(-1, *x.shape[:1], v.shape[1]) for v in pieces]


def plain_pieces(whole):
    cut = whole.shape[1] // 256 * 128
    chips = whole.reshape(4, 2, 2, 2, -1, whole.shape[1])
    left = chips[..., :cut].transpose(3, 1, 2, 0, 4, 5)
    right = chips[..., cut:].transpose(3, 2, 1, 0, 4, 5)
    return [v[core].reshape(16, -1, v.shape[-1]) for core in range(2) for v in (left, right)]


def columns(vector, r):
    return vector.reshape(-1, r).T


def table_of(vectors, n, r):
    parts = [v.reshape(n, -1, r).transpose(0, 2, 1).reshape(n * r, -1) for v in vectors]
    return jnp.concatenate(parts, axis=1)


def local(
    n,
    tokens,
    cotangent,
    w_qkv,
    q_bias,
    v_bias,
    w_out,
    out_bias,
    attn_gain,
    attn_shift,
    w_up,
    up_bias,
    w_down,
    down_bias,
    mlp_gain,
    mlp_shift,
):
    rows, width = tokens.shape
    r = w_qkv.shape[0]
    wide = w_up.shape[1] // width
    vectors = (
        q_bias, v_bias, out_bias, attn_gain, attn_shift, down_bias, mlp_gain, mlp_shift, up_bias,
    )
    small = jnp.concatenate([columns(v, r) for v in vectors], axis=1)
    small = jnp.pad(small, ((0, 0), (0, 128 - small.shape[1])))
    first = jnp.concatenate([w_qkv, small], axis=1)
    if n == CHUNKS:
        blocks = [w_up[:, j * width : (j + 1) * width] for j in range(wide)]
        held = gather(jnp.concatenate(blocks + [w_down, w_out], axis=0))
        held = held.reshape(CHUNKS, -1, width)
        pieces = gather_pieces(first, n)
        scatter, me = Scatter, lax.axis_index("dp")
    else:
        up = gather(w_up).reshape(CHUNKS, width // CHUNKS, wide, width).transpose(0, 2, 1, 3)
        up = up.reshape(CHUNKS, wide * width // CHUNKS, width)
        down = gather(w_down).reshape(CHUNKS, wide * width // CHUNKS, width)
        out = gather(w_out).reshape(CHUNKS, width // CHUNKS, width)
        held = jnp.concatenate([up, down, out], axis=1)
        pieces = plain_pieces(gather(first))
        scatter, me = PlainScatter, jnp.int32(0)
    core = (me & 1).reshape(1)
    me = me.reshape(1)
    tokens_t, *pieces = tie(tokens.T, *pieces)

    qkv, w_full, table = project(me, tokens, pieces)
    ob, g1, s1, db, g2, s2 = [table[j : j + 1] for j in range(2, 8)]
    ub = table[8 : 8 + wide].reshape(wide, CHUNKS, -1).transpose(1, 0, 2).reshape(1, -1)

    ctx, lse = attend(qkv, width)
    hat1, rstd1, n1_low = out_norm(ctx, held, ob, tokens, g1, s1)
    act, slope = up_gelu(n1_low, held, ub)
    layer_out, dh2, dm, d_g2, d_s2, d_db = down_norm(
        act, held, db, hat1, g1, s1, g2, s2, cotangent
    )

    down_sum = scatter(*down_grad(core, act, dm), n, w_down.shape[0])
    du, up_keep, up_send, d_ub = up_back(core, dm, held, slope, n1_low)
    up_sum = scatter(up_keep, up_send, n, r)
    du = down_sum.halve(du)
    dh1, da, d_g1, d_s1, d_ob = norm_back(du, held, dh2, hat1, rstd1, g1)
    dctx = context_back(da, held)
    dctx = down_sum.halve(dctx)
    dctx = up_sum.halve(dctx)
    pairs = width // 128

    def back(start, count):
        return attend_back(qkv, ctx, dctx, lse, width, start, count)

    first, sq0, sv0 = back(0, 3)
    first = down_sum.column_one(first)
    keep, send = attn_grad(core, tokens_t, [first], [ctx, da], "out")
    keep, dctx = up_sum.halve(keep, dctx)
    early_sum = scatter(keep, send, n, r)
    second, sq1, sv1 = back(3, 3)
    second, dctx = down_sum.column_two(second, dctx)
    second, dctx = up_sum.column_one(second, dctx)
    second, dctx = early_sum.halve(second, dctx)
    third, sq2, sv2 = back(6, pairs - 6)
    third = early_sum.halve(third)
    third = up_sum.column_two(third)
    d_qb = jnp.concatenate([sq0, sq1, sq2], axis=1)
    d_vb = jnp.concatenate([sv0, sv1, sv2], axis=1)
    d_small = table_of([d_qb, d_vb, d_ob, d_g1, d_s1, d_db, d_g2, d_s2, d_ub], CHUNKS, width // CHUNKS)
    d_small = jnp.pad(d_small, ((0, 0), (0, 128 - d_small.shape[1]))).astype(BF16)
    keep, send = attn_grad(core, tokens_t, [second, third], [d_small], "small")
    late_sum = scatter(keep, send, n, r)
    dh1 = late_sum.halve(dh1)
    input_grad = input_back([first, second, third], w_full, dh1)
    input_grad = late_sum.halve(input_grad)
    input_grad = early_sum.column(input_grad)
    late_sum.column()

    early, late = early_sum.result(), late_sum.result()
    qkv_cols = 3 * 384
    d_qkv = jnp.concatenate([early[:, :qkv_cols], late[:, : 3 * width - qkv_cols]], axis=1)
    d_qkv = d_qkv.reshape(r, pairs, 3, 128).transpose(0, 2, 1, 3).reshape(r, 3 * width)
    d_out = early[:, qkv_cols:]
    d_small = late[:, 3 * width - qkv_cols :]

    def vector(start, k=1):
        return d_small[:, start : start + k].T.reshape(-1)

    d_qb, d_vb, d_ob, d_g1, d_s1, d_db, d_g2, d_s2 = [vector(j) for j in range(8)]
    d_ub = d_small[:, 8 : 8 + wide]
    d_ub = d_ub.T.reshape(-1)
    return (
        layer_out, input_grad, d_qkv, d_qb, d_vb, d_out, d_ob, d_g1, d_s1,
        up_sum.result(), d_ub, down_sum.result(), d_db, d_g2, d_s2,
    )


def solution(mesh):
    flat, square = P("dp"), P("dp", None)
    in_specs = (
        square, square, square, flat, flat, square, flat, flat, flat,
        square, flat, square, flat, flat, flat,
    )
    return jax.shard_map(
        functools.partial(local, mesh.shape["dp"]),
        mesh=mesh,
        in_specs=in_specs,
        out_specs=in_specs,
        check_vma=False,
    )
```

time: 1080 us -> 497 us (0.46)
  matrix products: 307 us -> 0 us
  waiting for transfers between devices: 454 us -> 151 us
  Pallas kernels: 0 us -> 211 us
  blocking collectives: 126 us -> 0 us
  local copies, waits for them, and re-layouts: 111 us -> 22.2 us
  starting transfers between devices: 0.31 us -> 39.4 us
  other arithmetic: 63.5 us -> 48.5 us
    reduce_scatter x3 -> x0, waiting for transfers between devices: 372 us -> none  [the longest x1 188 us: local(): lax.psum_scatter(mlp_terms[2], 'dp', scatter_dimension=0, tiled=True)]
    dot_general x26 -> x0, matrix products: 307 us -> none  [the longest x1 48.3 us: local(): jnp.dot(normed_low, full_up, preferred_element_type=jnp.float32)]
    pallas_call x0 -> x15, Pallas kernels: none -> 211 us  [the longest x3 33.2 us: attend_back(): pl.pallas_call(attend_back_kernel, grid=(n_pairs, count), in_specs=[pl.Bl...]
    ppermute x0 -> x39, waiting for transfers between devices: none -> 110 us  [exchange(): return lax.ppermute(x, 'dp', [(i, i ^ mask) for i in range(n)])]
    unnamed x2 -> x0, blocking collectives: 85.2 us -> none
    unnamed x9 -> x1, waiting for transfers between devices: 51.1 us -> 0.02 us
    all_gather x1 -> x0, blocking collectives: 40.3 us -> none  [local(): lax.all_gather(up_bias, 'dp', axis=0, tiled=True)]
    ppermute x0 -> x39, starting transfers between devices: none -> 39.3 us  [exchange(): return lax.ppermute(x, 'dp', [(i, i ^ mask) for i in range(n)])]
  transfers between devices with their start and end apart: 8 -> 40, of which waited for: 5 -> 19; matrix products, arithmetic and copies ran while one was open for 35% -> 9% of each run, Pallas kernels for 0% -> 28%
where the time goes in v1:
time: 497 us; the launch traced here: 487 us
  Pallas kernels  211 us (42%)
  waiting for transfers between devices  151 us (30%)
  other arithmetic  48.5 us (10%)
  starting transfers between devices  39.4 us (8%)
  local copies, waits for them, and re-layouts  22.2 us (4%)
  between operations  15.1 us (3%)
    ppermute x39, waiting for transfers between devices, exchange(): return lax.ppermute(x, 'dp', [(i, i ^ mask) for i in range(n)])  110 us
    all_gather x1, waiting for transfers between devices, gather(): return lax.all_gather(x, 'dp', axis=0, tiled=True)  41 us
    ppermute x39, starting transfers between devices, exchange(): return lax.ppermute(x, 'dp', [(i, i ^ mask) for i in range(n)])  39.3 us
    convert_element_type x18, other arithmetic, halve(): self.part(side, bit, which).astype(BF16)  34.7 us
    pallas_call x3, Pallas kernels, attend_back(): pl.pallas_call(attend_back_kernel, grid=(n_pairs, count), in_specs=[pl.Bl...  33.2 us
    pallas_call x1, Pallas kernels, up_gelu(): pl.pallas_call(up_kernel, grid=(cols // block,), in_specs=[full_spec((row...  26.1 us
    pallas_call x1, Pallas kernels, up_back(): pl.pallas_call(up_back_kernel, grid=(deep // block,), in_specs=[SCALAR, f...  22.9 us
    pallas_call x1, Pallas kernels, attend(): pl.pallas_call(attend_kernel, grid=(pairs, count), in_specs=[pl.BlockSpec...  22.6 us
  transfers between devices with their start and end apart: 40, of which 19 were waited for; matrix products, arithmetic and copies ran while one was open for 9% of the time, Pallas kernels for 28%

profile of v1, /device:TPU:0, one launch (start us, length us, event | category | flops | bytes accessed | tf_op | source)
XLA Modules:
  0.0 487.5 jit_solution(14735433036827403012)
XLA Ops:
  15.9 3.1 collective-permute-start
  19.0 2.6 collective-permute-start.1
  21.7 6.0 %collective-permute-done = bf16[32,3200]{1,0:T(8,128)(2,1)S(1)} collective-permute-done((bf16[32,3200]{1,0:T(8,128)(2,1)S(1)}, bf16[32,3200]{1,0:T(8,128)(2,1)S(1)}, u32[]{:S(2)}, u32[]{:S(2)}) %collective-permute-start) | collective-permute-done | bytes 204832 | tf_op jit(solution)/shard_map/ppermute | solution.py:606
  27.7 13.5 %collective-permute-done.1 = bf16[32,3200]{1,0:T(8,128)(2,1)S(1)} collective-permute-done((bf16[32,3200]{1,0:T(8,128)(2,1)S(1)}, bf16[32,3200]{1,0:T(8,128)(2,1)S(1)}, u32[]{:S(2)}, u32[]{:S(2)}) %collective-permute-start.1) | collective-permute-done | bytes 204832 | tf_op jit(solution)/shard_map/ppermute | solution.py:606
  44.6 5.3 %collective-permute-done.5 = bf16[128,1664]{1,0:T(8,128)(2,1)S(1)} collective-permute-done((bf16[128,1664]{1,0:T(8,128)(2,1)S(1)}, bf16[128,1664]{1,0:T(8,128)(2,1)S(1)}, u32[]{:S(2)}, u32[]{:S(2)}) %collective-permute-start.5) | collective-permute-done | bytes 426016 | tf_op jit(solution)/shard_map/ppermute | solution.py:606
  54.1 27.5 %collective-permute-done.6 = bf16[256,1664]{1,0:T(8,128)(2,1)S(1)} collective-permute-done((bf16[256,1664]{1,0:T(8,128)(2,1)S(1)}, bf16[256,1664]{1,0:T(8,128)(2,1)S(1)}, u32[]{:S(2)}, u32[]{:S(2)}) %collective-permute-start.6) | collective-permute-done | bytes 852000 | tf_op jit(solution)/shard_map/ppermute | solution.py:606
  82.5 4.0 copy.169
  87.8 15.3 %project.1 = (bf16[1024,3072]{1,0:T(8,128)(2,1)}, bf16[1024,3200]{1,0:T(8,128)(2,1)}, f32[16,1024]{1,0:T(8,128)S(1)}) custom-call(s32[1]{0:T(128)} %bitcast.me_ref, bf16[1024,1024]{1,0:T(8,128)(2,1)} %x_ref.3, bf16[16,32,1536]{2,1,0:T(8,128)(2,1)S(1)} %bitcast.260, bf16[16,32,1664]{2,1,0:T(8,128)(2,1)S(1)} %bitcast.259, ...), custom_call_target="tpu_custom_call" | custom-call | flops 128849016 | bytes 419430 | tf_op jit(solution)/shard_map/project/pallas_call | solution.py:101
  103.4 22.6 %attend.1 = (bf16[1024,1024]{1,0:T(8,128)(2,1)S(1)}, f32[8,2,2,512]{3,2,1,0:T(2,128)S(1)}) custom-call(bf16[1024,3072]{1,0:T(8,128)(2,1)} %get-tuple-element.198.q_ref.k_ref.v_ref, bf16[1024,3072]{1,0:T(8,128)(2,1)} %get-tuple-element.198.q_ref.k_ref.v_ref, bf16[1024,3072]{1,0:T(8,128)(2,1)} %get-tuple-element.198.q_ref.k_ref.v_ref), custom_call_target="tpu_custom_call" | custom-call | flops 171798688 | bytes 167772 | tf_op jit(solution)/shard_map/attend/pallas_call | solution.py:147
  126.0 41.0 %all-gather.2.cloned.1.call-done = bf16[9216,1024]{1,0:T(8,128)(2,1)} async-done(((bf16[288,1024]{1,0:T(8,128)(2,1)}), bf16[9216,1024]{1,0:T(8,128)(2,1)}) %all-gather.2.cloned.1.call-update) | async-done | bytes 18874384 | tf_op jit(solution)/shard_map/all_gather | solution.py:719
  167.0 7.4 %out_norm.1 = (f32[1024,1024]{1,0:T(8,128)}, f32[1024,1]{1,0:T(8,128)S(1)}, bf16[1024,1024]{1,0:T(8,128)(2,1)S(1)}) custom-call(bf16[1024,1024]{1,0:T(8,128)(2,1)S(1)} %get-tuple-element.199.c_ref.refs_1_, bf16[32,288,1024]{2,1,0:T(8,128)(2,1)} %bitcast.261, f32[1,1024]{1,0:T(1,128)S(1)} %get-tuple-element.470.b_ref, bf16[1024,1024]{1,0:T(8,128)(2,1)} %x_ref.3, ...), custom_call_target="tpu_custom_call" | custom-call | flops 42949672 | bytes 293601 | tf_op jit(solution)/shard_map/out_norm/pallas_call | solution.py:263
  174.4 26.1 %up_gelu.1 = (bf16[1024,4096]{1,0:T(8,128)(2,1)}, bf16[1024,4096]{1,0:T(8,128)(2,1)}) custom-call(bf16[1024,1024]{1,0:T(8,128)(2,1)S(1)} %get-tuple-element.201.x_ref, bf16[32,288,1024]{2,1,0:T(8,128)(2,1)} %bitcast.262, f32[1,4096]{1,0:T(1,128)S(1)} %reshape.415.b_ref), custom_call_target="tpu_custom_call" | custom-call | flops 171798688 | bytes 503316 | tf_op jit(solution)/shard_map/up_gelu/pallas_call | solution.py:312
  200.5 18.7 %down_norm.1 = (bf16[1024,1024]{1,0:T(8,128)(2,1)}, f32[1024,1024]{1,0:T(8,128)}, bf16[1024,1024]{1,0:T(8,128)(2,1)S(1)}, f32[1,1024]{1,0:T(1,128)S(1)}, f32[1,1024]{1,0:T(1,128)S(1)}, /*index=5*/f32[1,1024]{1,0:T(1,128)S(1)}) custom-call(bf16[1024,4096]{1,0:T(8,128)(2,1)} %get-tuple-element.202.a_ref, bf16[32,288,1024]{2,1,0:T(8,128)(2,1)} %bitcast.263, ...), custom_call_target="tpu_custom_call" | custom-call | flops 171798688 | bytes 629145 | tf_op jit(solution)/shard_map/down_norm/pallas_call | solution.py:365
  219.2 13.7 %down_grad.1 = (bf16[2,1024,1024]{2,1,0:T(8,128)(2,1)}, bf16[2,1024,1024]{2,1,0:T(8,128)(2,1)}) custom-call(s32[1]{0:T(128)} %bitcast.17.core_ref, bf16[1024,4096]{1,0:T(8,128)(2,1)} %get-tuple-element.202.a_ref, bf16[1024,1024]{1,0:T(8,128)(2,1)S(1)} %get-tuple-element.205.dm_ref.b_ref), custom_call_target="tpu_custom_call" | custom-call | flops 171798688 | bytes 377487 | tf_op jit(solution)/shard_map/down_grad/pallas_call | solution.py:407
  233.2 22.9 %up_back.1 = (bf16[1024,4096]{1,0:T(8,128)(2,1)}, bf16[2,256,4096]{2,1,0:T(8,128)(2,1)}, bf16[2,256,4096]{2,1,0:T(8,128)(2,1)}, f32[1,4096]{1,0:T(1,128)S(1)}) custom-call(s32[1]{0:T(128)} %bitcast.17.core_ref, bf16[1024,1024]{1,0:T(8,128)(2,1)S(1)} %get-tuple-element.205.dm_ref.b_ref, bf16[32,288,1024]{2,1,0:T(8,128)(2,1)} %bitcast.264, ...), custom_call_target="tpu_custom_call" | custom-call | flops 343597376 | bytes 754974 | tf_op jit(solution)/shard_map/up_back/pallas_call | solution.py:483
  256.3 3.3 fusion.1
  264.4 17.3 %norm_back.1 = (f32[1024,1024]{1,0:T(8,128)}, bf16[1024,1024]{1,0:T(8,128)(2,1)S(1)}, f32[1,1024]{1,0:T(1,128)S(1)}, f32[1,1024]{1,0:T(1,128)S(1)}, f32[1,1024]{1,0:T(1,128)S(1)}) custom-call(bf16[1024,4096]{1,0:T(8,128)(2,1)} %get-tuple-element.221.du_ref, bf16[32,288,1024]{2,1,0:T(8,128)(2,1)} %bitcast.265, f32[1024,1024]{1,0:T(8,128)} %get-tuple-element.222.dh2_ref, ...), custom_call_target="tpu_custom_call" | custom-call | flops 171798688 | bytes 629145 | tf_op jit(solution)/shard_map/norm_back/pallas_call | solution.py:541
  281.7 4.9 %context_back.1.d_ref = bf16[1024,1024]{1,0:T(8,128)(2,1)S(1)} custom-call(bf16[1024,1024]{1,0:T(8,128)(2,1)S(1)} %get-tuple-element.224.da_ref.refs_2_, bf16[32,288,1024]{2,1,0:T(8,128)(2,1)} %bitcast.266), custom_call_target="tpu_custom_call" | custom-call | flops 42949672 | bytes 125829 | tf_op jit(solution)/shard_map/context_back/pallas_call | solution.py:563
  291.8 3.6 fusion.3
  295.5 3.3 add_convert_fusion.2
  304.4 12.7 %attend_back.3 = (bf16[1024,1152]{1,0:T(8,128)(2,1)}, f32[1,384]{1,0:T(1,128)S(1)}, f32[1,384]{1,0:T(1,128)S(1)}) custom-call(bf16[1024,3072]{1,0:T(8,128)(2,1)} %get-tuple-element.198.q_ref.k_ref.v_ref, bf16[1024,3072]{1,0:T(8,128)(2,1)} %get-tuple-element.198.q_ref.k_ref.v_ref, bf16[1024,3072]{1,0:T(8,128)(2,1)} %get-tuple-element.198.q_ref.k_ref.v_ref, ...), custom_call_target="tpu_custom_call" | custom-call | flops 161061280 | bytes 125829 | tf_op jit(solution)/shard_map/attend_back/pallas_call | solution.py:218
  317.1 17.7 %collective-permute-done.15 = bf16[4,64,1024]{2,1,0:T(8,128)(2,1)} collective-permute-done((bf16[4,64,1024]{2,1,0:T(8,128)(2,1)}, bf16[4,64,1024]{2,1,0:T(8,128)(2,1)}, u32[]{:S(2)}, u32[]{:S(2)}) %collective-permute-start.15) | collective-permute-done | bytes 524320 | tf_op jit(solution)/shard_map/ppermute | solution.py:606
  339.8 9.2 %attn_grad.2 = (bf16[2,256,2176]{2,1,0:T(8,128)(2,1)}, bf16[2,256,2176]{2,1,0:T(8,128)(2,1)}) custom-call(s32[1]{0:T(128)} %bitcast.17.core_ref, bf16[1024,1024]{1,0:T(8,128)(2,1)S(1)} %bitcast.256, bf16[1024,1152]{1,0:T(8,128)(2,1)} %get-tuple-element.253.refs_0_, bf16[1024,1024]{1,0:T(8,128)(2,1)S(1)} %get-tuple-element.199.c_ref.refs_1_, ...), custom_call_target="tpu_custom_call" | custom-call | flops 91268056 | bytes 220200 | tf_op jit(solution)/shard_map/attn_grad/pallas_call | solution.py:451
  357.9 12.4 %attend_back.4 = (bf16[1024,1152]{1,0:T(8,128)(2,1)}, f32[1,384]{1,0:T(1,128)S(1)}, f32[1,384]{1,0:T(1,128)S(1)}) custom-call(bf16[1024,3072]{1,0:T(8,128)(2,1)} %get-tuple-element.198.q_ref.k_ref.v_ref, bf16[1024,3072]{1,0:T(8,128)(2,1)} %get-tuple-element.198.q_ref.k_ref.v_ref, bf16[1024,3072]{1,0:T(8,128)(2,1)} %get-tuple-element.198.q_ref.k_ref.v_ref, ...), custom_call_target="tpu_custom_call" | custom-call | flops 161061280 | bytes 125829 | tf_op jit(solution)/shard_map/attend_back/pallas_call | solution.py:218
  382.7 8.2 %attend_back.5 = (bf16[1024,768]{1,0:T(8,128)(2,1)S(1)}, f32[1,256]{1,0:T(1,128)S(1)}, f32[1,256]{1,0:T(1,128)S(1)}) custom-call(bf16[1024,3072]{1,0:T(8,128)(2,1)} %get-tuple-element.198.q_ref.k_ref.v_ref, bf16[1024,3072]{1,0:T(8,128)(2,1)} %get-tuple-element.198.q_ref.k_ref.v_ref, bf16[1024,3072]{1,0:T(8,128)(2,1)} %get-tuple-element.198.q_ref.k_ref.v_ref, ...), custom_call_target="tpu_custom_call" | custom-call | flops 107374184 | bytes 83886 | tf_op jit(solution)/shard_map/attend_back/pallas_call | solution.py:218
  401.1 6.2 %collective-permute-done.25 = bf16[2,32,4096]{2,1,0:T(8,128)(2,1)} collective-permute-done((bf16[2,32,4096]{2,1,0:T(8,128)(2,1)}, bf16[2,32,4096]{2,1,0:T(8,128)(2,1)}, u32[]{:S(2)}, u32[]{:S(2)}) %collective-permute-start.25) | collective-permute-done | bytes 524320 | tf_op jit(solution)/shard_map/ppermute | solution.py:606
  409.2 8.2 %attn_grad.3 = (bf16[2,256,2048]{2,1,0:T(8,128)(2,1)S(1)}, bf16[2,256,2048]{2,1,0:T(8,128)(2,1)}) custom-call(s32[1]{0:T(128)} %bitcast.17.core_ref, bf16[1024,1024]{1,0:T(8,128)(2,1)} %bitcast.255, bf16[1024,1152]{1,0:T(8,128)(2,1)} %get-tuple-element.306.refs_0_.refs_1_, bf16[1024,768]{1,0:T(8,128)(2,1)S(1)} %copy-done.7, bf16[1024,128]{1,0:T(8,128)(2,1)S(1)} %pad.10.refs_2_), custom_call_target="tpu_custom_call" | custom-call | flops 85899344 | bytes 209715 | tf_op jit(solution)/shard_map/attn_grad/pallas_call | solution.py:451
  418.8 9.0 %collective-permute-done.38 = bf16[128,1024]{1,0:T(8,128)(2,1)} collective-permute-done((bf16[128,1024]{1,0:T(8,128)(2,1)}, bf16[128,1024]{1,0:T(8,128)(2,1)}, u32[]{:S(2)}, u32[]{:S(2)}) %collective-permute-start.38) | collective-permute-done | bytes 262176 | tf_op jit(solution)/shard_map/ppermute | solution.py:606
  438.6 11.5 %input_back.1 = bf16[1024,1024]{1,0:T(8,128)(2,1)} custom-call(bf16[1024,1152]{1,0:T(8,128)(2,1)S(1)} %copy-done.4, bf16[1024,1152]{1,0:T(8,128)(2,1)} %get-tuple-element.306.refs_0_.refs_1_, bf16[1024,768]{1,0:T(8,128)(2,1)S(1)} %copy-done.7, bf16[1024,3200]{1,0:T(8,128)(2,1)} %get-tuple-element.339.refs_3_, f32[1024,1024]{1,0:T(8,128)} %get-tuple-element.340.refs_4_), custom_call_target="tpu_custom_call" | custom-call | flops 128849016 | bytes 377487 | tf_op jit(solution)/shard_map/input_back/pallas_call | solution.py:592
  455.2 2.6 collective-permute-start.31
  463.4 5.4 %collective-permute-done.30 = bf16[32,2176]{1,0:T(8,128)(2,1)S(1)} collective-permute-done((bf16[32,2176]{1,0:T(8,128)(2,1)S(1)}, bf16[32,2176]{1,0:T(8,128)(2,1)S(1)}, u32[]{:S(2)}, u32[]{:S(2)}) %collective-permute-start.30) | collective-permute-done | bytes 139296 | tf_op jit(solution)/shard_map/ppermute | solution.py:606
  469.5 7.8 %collective-permute-done.35 = bf16[32,2048]{1,0:T(8,128)(2,1)S(1)} collective-permute-done((bf16[32,2048]{1,0:T(8,128)(2,1)S(1)}, bf16[32,2048]{1,0:T(8,128)(2,1)S(1)}, u32[]{:S(2)}, u32[]{:S(2)}) %collective-permute-start.35) | collective-permute-done | bytes 131104 | tf_op jit(solution)/shard_map/ppermute | solution.py:606
  (219 shorter events, 99.1 us)
Async XLA Ops:
  7.2 159.8 %all-gather.2.cloned.1.call-start = ((), (), s32[]{:S(2)}) async-start(), calls=%async_computation | async-start | bytes 19464192 | tf_op jit(solution)/shard_map/all_gather | solution.py:719
  15.9 11.8 %collective-permute-start = (bf16[32,3200]{1,0:T(8,128)(2,1)S(1)}, bf16[32,3200]{1,0:T(8,128)(2,1)S(1)}, u32[]{:S(2)}, u32[]{:S(2)}) collective-permute-start(bf16[32,3200]{1,0:T(8,128)(2,1)S(1)} %fusion.35), channel_id=1, source_target_pairs={{0,8},{1,9},{2,10},{3,11},{4,12},{5,13},{6,14},{7,15},{8,0},{9,1},... | collective-permute-start | bytes 614408 | tf_op jit(solution)/shard_map/ppermute | solution.py:606
  19.0 22.3 %collective-permute-start.1 = (bf16[32,3200]{1,0:T(8,128)(2,1)S(1)}, bf16[32,3200]{1,0:T(8,128)(2,1)S(1)}, u32[]{:S(2)}, u32[]{:S(2)}) collective-permute-start(bf16[32,3200]{1,0:T(8,128)(2,1)S(1)} %fusion.35), channel_id=1, source_target_pairs={{0,16},{1,17},{2,18},{3,19},{4,20},{5,21},{6,22},{7,23},{8,24},{9,... | collective-permute-start | bytes 614408 | tf_op jit(solution)/shard_map/ppermute | solution.py:606
  21.6 19.7 %collective-permute-start.2 = (bf16[32,3200]{1,0:T(8,128)(2,1)S(1)}, bf16[32,3200]{1,0:T(8,128)(2,1)S(1)}, u32[]{:S(2)}, u32[]{:S(2)}) collective-permute-start(bf16[32,3200]{1,0:T(8,128)(2,1)S(1)} %fusion.35), channel_id=1, source_target_pairs={{0,24},{1,25},{2,26},{3,27},{4,28},{5,29},{6,30},{7,31},{8,16},{9,... | collective-permute-start | bytes 614408 | tf_op jit(solution)/shard_map/ppermute | solution.py:606
  43.1 10.0 %collective-permute-start.3 = (bf16[128,1536]{1,0:T(8,128)(2,1)S(1)}, bf16[128,1536]{1,0:T(8,128)(2,1)S(1)}, u32[]{:S(2)}, u32[]{:S(2)}) collective-permute-start(bf16[128,1536]{1,0:T(8,128)(2,1)S(1)} %pad_maximum_fusion.5), channel_id=1, source_target_pairs={{0,2},{1,3},{2,0},{3,1},{4,6},{5,7},{6,4},{7,5},{8,10},{9,11},{10,... | collective-permute-start | bytes 1179656 | tf_op jit(solution)/shard_map/ppermute | solution.py:606
  50.1 31.6 %collective-permute-start.6 = (bf16[256,1664]{1,0:T(8,128)(2,1)S(1)}, bf16[256,1664]{1,0:T(8,128)(2,1)S(1)}, u32[]{:S(2)}, u32[]{:S(2)}) collective-permute-start(bf16[256,1664]{1,0:T(8,128)(2,1)S(1)} %get-tuple-element.437), channel_id=1, source_target_pairs={{0,2},{1,3},{2,0},{3,1},{4,6},{5,7},{6,4},{7,5},{8,10},{9,11},{10,... | collective-permute-start | bytes 2555912 | tf_op jit(solution)/shard_map/ppermute | solution.py:606
  53.1 28.7 %collective-permute-start.4 = (bf16[256,1536]{1,0:T(8,128)(2,1)S(1)}, bf16[256,1536]{1,0:T(8,128)(2,1)S(1)}, u32[]{:S(2)}, u32[]{:S(2)}) collective-permute-start(bf16[256,1536]{1,0:T(8,128)(2,1)S(1)} %get-tuple-element.439), channel_id=1, source_target_pairs={{0,4},{1,5},{2,6},{3,7},{4,0},{5,1},{6,2},{7,3},{8,12},{9,13},{10,... | collective-permute-start | bytes 2359304 | tf_op jit(solution)/shard_map/ppermute | solution.py:606
  232.9 23.4 %collective-permute-start.10 = (bf16[2,1024,1024]{2,1,0:T(8,128)(2,1)}, bf16[2,1024,1024]{2,1,0:T(8,128)(2,1)}, u32[]{:S(2)}, u32[]{:S(2)}) collective-permute-start(bf16[2,1024,1024]{2,1,0:T(8,128)(2,1)} %get-tuple-element.210), channel_id=1, source_target_pairs={{0,1},{1,0},{2,3},{3,2},{4,5},{5,4},{6,7},{7,6},{8,9},{9,8},{10,11... | collective-permute-start | bytes 12582920 | tf_op jit(solution)/shard_map/ppermute | solution.py:606
  256.1 35.7 %collective-permute-start.9 = (bf16[2,256,4096]{2,1,0:T(8,128)(2,1)}, bf16[2,256,4096]{2,1,0:T(8,128)(2,1)}, u32[]{:S(2)}, u32[]{:S(2)}) collective-permute-start(bf16[2,256,4096]{2,1,0:T(8,128)(2,1)} %get-tuple-element.208), channel_id=1, source_target_pairs={{0,1},{1,0},{2,3},{3,2},{4,5},{5,4},{6,7},{7,6},{8,9},{9,8},{10,11... | collective-permute-start | bytes 12582920 | tf_op jit(solution)/shard_map/ppermute | solution.py:606
  262.3 25.4 %collective-permute-start.11 = (bf16[8,64,1024]{2,1,0:T(8,128)(2,1)S(1)}, bf16[8,64,1024]{2,1,0:T(8,128)(2,1)S(1)}, u32[]{:S(2)}, u32[]{:S(2)}) collective-permute-start(bf16[8,64,1024]{2,1,0:T(8,128)(2,1)S(1)} %bitcast.291), channel_id=1, source_target_pairs={{0,4},{1,5},{2,6},{3,7},{4,0},{5,1},{6,2},{7,3},{8,12},{9,13},{10,... | collective-permute-start | bytes 3145736 | tf_op jit(solution)/shard_map/ppermute | solution.py:606
  263.8 25.1 %collective-permute-start.12 = (bf16[8,64,1024]{2,1,0:T(8,128)(2,1)S(1)}, bf16[8,64,1024]{2,1,0:T(8,128)(2,1)S(1)}, u32[]{:S(2)}, u32[]{:S(2)}) collective-permute-start(bf16[8,64,1024]{2,1,0:T(8,128)(2,1)S(1)} %get-tuple-element.220), channel_id=1, source_target_pairs={{0,2},{1,3},{2,0},{3,1},{4,6},{5,7},{6,4},{7,5},{8,10},{9,11},{10,... | collective-permute-start | bytes 3145736 | tf_op jit(solution)/shard_map/ppermute | solution.py:606
  298.8 50.3 %collective-permute-start.13 = (bf16[8,16,4096]{2,1,0:T(8,128)(2,1)}, bf16[8,16,4096]{2,1,0:T(8,128)(2,1)}, u32[]{:S(2)}, u32[]{:S(2)}) collective-permute-start(bf16[8,16,4096]{2,1,0:T(8,128)(2,1)} %bitcast.36), channel_id=1, source_target_pairs={{0,4},{1,5},{2,6},{3,7},{4,0},{5,1},{6,2},{7,3},{8,12},{9,13},{10,... | collective-permute-start | bytes 3145736 | tf_op jit(solution)/shard_map/ppermute | solution.py:606
  299.3 49.7 %collective-permute-start.14 = (bf16[8,16,4096]{2,1,0:T(8,128)(2,1)}, bf16[8,16,4096]{2,1,0:T(8,128)(2,1)}, u32[]{:S(2)}, u32[]{:S(2)}) collective-permute-start(bf16[8,16,4096]{2,1,0:T(8,128)(2,1)} %get-tuple-element.239), channel_id=1, source_target_pairs={{0,2},{1,3},{2,0},{3,1},{4,6},{5,7},{6,4},{7,5},{8,10},{9,11},{10,... | collective-permute-start | bytes 3145736 | tf_op jit(solution)/shard_map/ppermute | solution.py:606
  300.7 34.1 %collective-permute-start.15 = (bf16[4,64,1024]{2,1,0:T(8,128)(2,1)}, bf16[4,64,1024]{2,1,0:T(8,128)(2,1)}, u32[]{:S(2)}, u32[]{:S(2)}) collective-permute-start(bf16[4,64,1024]{2,1,0:T(8,128)(2,1)} %get-tuple-element.242), channel_id=1, source_target_pairs={{0,2},{1,3},{2,0},{3,1},{4,6},{5,7},{6,4},{7,5},{8,10},{9,11},{10,... | collective-permute-start | bytes 1572872 | tf_op jit(solution)/shard_map/ppermute | solution.py:606
  301.4 33.4 %collective-permute-start.16 = (bf16[4,64,1024]{2,1,0:T(8,128)(2,1)}, bf16[4,64,1024]{2,1,0:T(8,128)(2,1)}, u32[]{:S(2)}, u32[]{:S(2)}) collective-permute-start(bf16[4,64,1024]{2,1,0:T(8,128)(2,1)} %get-tuple-element.244), channel_id=1, source_target_pairs={{0,4},{1,5},{2,6},{3,7},{4,0},{5,1},{6,2},{7,3},{8,12},{9,13},{10,... | collective-permute-start | bytes 1572872 | tf_op jit(solution)/shard_map/ppermute | solution.py:606
  338.3 32.0 %collective-permute-start.20 = (bf16[2,128,1024]{2,1,0:T(8,128)(2,1)}, bf16[2,128,1024]{2,1,0:T(8,128)(2,1)}, u32[]{:S(2)}, u32[]{:S(2)}) collective-permute-start(bf16[2,128,1024]{2,1,0:T(8,128)(2,1)} %pad_maximum_fusion), channel_id=1, source_target_pairs={{0,16},{1,17},{2,18},{3,19},{4,20},{5,21},{6,22},{7,23},{8,24},{9,... | collective-permute-start | bytes 1572872 | tf_op jit(solution)/shard_map/ppermute | solution.py:606
  354.0 18.5 %collective-permute-start.18 = (bf16[4,16,4096]{2,1,0:T(8,128)(2,1)}, bf16[4,16,4096]{2,1,0:T(8,128)(2,1)S(1)}, u32[]{:S(2)}, u32[]{:S(2)}) collective-permute-start(bf16[4,16,4096]{2,1,0:T(8,128)(2,1)} %get-tuple-element.264), channel_id=1, source_target_pairs={{0,2},{1,3},{2,0},{3,1},{4,6},{5,7},{6,4},{7,5},{8,10},{9,11},{10,... | collective-permute-start | bytes 1572872 | tf_op jit(solution)/shard_map/ppermute | solution.py:606
  355.4 17.1 %collective-permute-start.19 = (bf16[4,16,4096]{2,1,0:T(8,128)(2,1)}, bf16[4,16,4096]{2,1,0:T(8,128)(2,1)S(1)}, u32[]{:S(2)}, u32[]{:S(2)}) collective-permute-start(bf16[4,16,4096]{2,1,0:T(8,128)(2,1)} %get-tuple-element.266), channel_id=1, source_target_pairs={{0,4},{1,5},{2,6},{3,7},{4,0},{5,1},{6,2},{7,3},{8,12},{9,13},{10,... | collective-permute-start | bytes 1572872 | tf_op jit(solution)/shard_map/ppermute | solution.py:606
  356.0 18.5 %collective-permute-start.17 = (bf16[2,256,2176]{2,1,0:T(8,128)(2,1)}, bf16[2,256,2176]{2,1,0:T(8,128)(2,1)}, u32[]{:S(2)}, u32[]{:S(2)}) collective-permute-start(bf16[2,256,2176]{2,1,0:T(8,128)(2,1)} %get-tuple-element.262), channel_id=1, source_target_pairs={{0,1},{1,0},{2,3},{3,2},{4,5},{5,4},{6,7},{7,6},{8,9},{9,8},{10,11... | collective-permute-start | bytes 6684680 | tf_op jit(solution)/shard_map/ppermute | solution.py:606
  379.1 15.3 %collective-permute-start.21 = (bf16[8,16,2176]{2,1,0:T(8,128)(2,1)}, bf16[8,16,2176]{2,1,0:T(8,128)(2,1)}, u32[]{:S(2)}, u32[]{:S(2)}) collective-permute-start(bf16[8,16,2176]{2,1,0:T(8,128)(2,1)} %bitcast.70), channel_id=1, source_target_pairs={{0,4},{1,5},{2,6},{3,7},{4,0},{5,1},{6,2},{7,3},{8,12},{9,13},{10,... | collective-permute-start | bytes 1671176 | tf_op jit(solution)/shard_map/ppermute | solution.py:606
  380.5 15.1 %collective-permute-start.22 = (bf16[8,16,2176]{2,1,0:T(8,128)(2,1)}, bf16[8,16,2176]{2,1,0:T(8,128)(2,1)}, u32[]{:S(2)}, u32[]{:S(2)}) collective-permute-start(bf16[8,16,2176]{2,1,0:T(8,128)(2,1)} %get-tuple-element.294), channel_id=1, source_target_pairs={{0,2},{1,3},{2,0},{3,1},{4,6},{5,7},{6,4},{7,5},{8,10},{9,11},{10,... | collective-permute-start | bytes 1671176 | tf_op jit(solution)/shard_map/ppermute | solution.py:606
  381.2 26.1 %collective-permute-start.25 = (bf16[2,32,4096]{2,1,0:T(8,128)(2,1)}, bf16[2,32,4096]{2,1,0:T(8,128)(2,1)}, u32[]{:S(2)}, u32[]{:S(2)}) collective-permute-start(bf16[2,32,4096]{2,1,0:T(8,128)(2,1)} %pad_maximum_fusion.2), channel_id=1, source_target_pairs={{0,16},{1,17},{2,18},{3,19},{4,20},{5,21},{6,22},{7,23},{8,24},{9,... | collective-permute-start | bytes 1572872 | tf_op jit(solution)/shard_map/ppermute | solution.py:606
  418.8 13.3 %collective-permute-start.26 = (bf16[2,256,2048]{2,1,0:T(8,128)(2,1)}, bf16[2,256,2048]{2,1,0:T(8,128)(2,1)}, u32[]{:S(2)}, u32[]{:S(2)}) collective-permute-start(bf16[2,256,2048]{2,1,0:T(8,128)(2,1)} %get-tuple-element.328), channel_id=1, source_target_pairs={{0,1},{1,0},{2,3},{3,2},{4,5},{5,4},{6,7},{7,6},{8,9},{9,8},{10,11... | collective-permute-start | bytes 6291464 | tf_op jit(solution)/shard_map/ppermute | solution.py:606
  429.9 21.1 %collective-permute-start.23 = (bf16[4,16,2176]{2,1,0:T(8,128)(2,1)S(1)}, bf16[4,16,2176]{2,1,0:T(8,128)(2,1)S(1)}, u32[]{:S(2)}, u32[]{:S(2)}) collective-permute-start(bf16[4,16,2176]{2,1,0:T(8,128)(2,1)S(1)} %copy-done.25), channel_id=1, source_target_pairs={{0,2},{1,3},{2,0},{3,1},{4,6},{5,7},{6,4},{7,5},{8,10},{9,11},{10,... | collective-permute-start | bytes 835592 | tf_op jit(solution)/shard_map/ppermute | solution.py:606
  431.3 19.7 %collective-permute-start.24 = (bf16[4,16,2176]{2,1,0:T(8,128)(2,1)}, bf16[4,16,2176]{2,1,0:T(8,128)(2,1)S(1)}, u32[]{:S(2)}, u32[]{:S(2)}) collective-permute-start(bf16[4,16,2176]{2,1,0:T(8,128)(2,1)} %get-tuple-element.305), channel_id=1, source_target_pairs={{0,4},{1,5},{2,6},{3,7},{4,0},{5,1},{6,2},{7,3},{8,12},{9,13},{10,... | collective-permute-start | bytes 835592 | tf_op jit(solution)/shard_map/ppermute | solution.py:606
  435.8 15.0 %collective-permute-start.27 = (bf16[8,16,2048]{2,1,0:T(8,128)(2,1)S(1)}, bf16[8,16,2048]{2,1,0:T(8,128)(2,1)S(1)}, u32[]{:S(2)}, u32[]{:S(2)}) collective-permute-start(bf16[8,16,2048]{2,1,0:T(8,128)(2,1)S(1)} %bitcast.297), channel_id=1, source_target_pairs={{0,4},{1,5},{2,6},{3,7},{4,0},{5,1},{6,2},{7,3},{8,12},{9,13},{10,... | collective-permute-start | bytes 1572872 | tf_op jit(solution)/shard_map/ppermute | solution.py:606
  437.1 13.6 %collective-permute-start.28 = (bf16[8,16,2048]{2,1,0:T(8,128)(2,1)S(1)}, bf16[8,16,2048]{2,1,0:T(8,128)(2,1)S(1)}, u32[]{:S(2)}, u32[]{:S(2)}) collective-permute-start(bf16[8,16,2048]{2,1,0:T(8,128)(2,1)S(1)} %get-tuple-element.338), channel_id=1, source_target_pairs={{0,2},{1,3},{2,0},{3,1},{4,6},{5,7},{6,4},{7,5},{8,10},{9,11},{10,... | collective-permute-start | bytes 1572872 | tf_op jit(solution)/shard_map/ppermute | solution.py:606
  455.0 13.7 %collective-permute-start.30 = (bf16[32,2176]{1,0:T(8,128)(2,1)S(1)}, bf16[32,2176]{1,0:T(8,128)(2,1)S(1)}, u32[]{:S(2)}, u32[]{:S(2)}) collective-permute-start(bf16[32,2176]{1,0:T(8,128)(2,1)S(1)} %pad_maximum_fusion.10), channel_id=1, source_target_pairs={{0,16},{1,17},{2,18},{3,19},{4,20},{5,21},{6,22},{7,23},{8,24},{9,... | collective-permute-start | bytes 417800 | tf_op jit(solution)/shard_map/ppermute | solution.py:606
  455.2 13.5 %collective-permute-start.31 = (bf16[32,2176]{1,0:T(8,128)(2,1)S(1)}, bf16[32,2176]{1,0:T(8,128)(2,1)S(1)}, u32[]{:S(2)}, u32[]{:S(2)}) collective-permute-start(bf16[32,2176]{1,0:T(8,128)(2,1)S(1)} %pad_maximum_fusion.11), channel_id=1, source_target_pairs={{0,24},{1,25},{2,26},{3,27},{4,28},{5,29},{6,30},{7,31},{8,16},{9,... | collective-permute-start | bytes 417800 | tf_op jit(solution)/shard_map/ppermute | solution.py:606
  458.9 10.6 %collective-permute-start.34 = (bf16[32,2048]{1,0:T(8,128)(2,1)S(1)}, bf16[32,2048]{1,0:T(8,128)(2,1)S(1)}, u32[]{:S(2)}, u32[]{:S(2)}) collective-permute-start(bf16[32,2048]{1,0:T(8,128)(2,1)S(1)} %pad_maximum_fusion.12), channel_id=1, source_target_pairs={{0,8},{1,9},{2,10},{3,11},{4,12},{5,13},{6,14},{7,15},{8,0},{9,1},... | collective-permute-start | bytes 393224 | tf_op jit(solution)/shard_map/ppermute | solution.py:606
  460.4 16.9 %collective-permute-start.35 = (bf16[32,2048]{1,0:T(8,128)(2,1)S(1)}, bf16[32,2048]{1,0:T(8,128)(2,1)S(1)}, u32[]{:S(2)}, u32[]{:S(2)}) collective-permute-start(bf16[32,2048]{1,0:T(8,128)(2,1)S(1)} %pad_maximum_fusion.13), channel_id=1, source_target_pairs={{0,16},{1,17},{2,18},{3,19},{4,20},{5,21},{6,22},{7,23},{8,24},{9,... | collective-permute-start | bytes 393224 | tf_op jit(solution)/shard_map/ppermute | solution.py:606
  463.0 14.4 %collective-permute-start.36 = (bf16[32,2048]{1,0:T(8,128)(2,1)S(1)}, bf16[32,2048]{1,0:T(8,128)(2,1)S(1)}, u32[]{:S(2)}, u32[]{:S(2)}) collective-permute-start(bf16[32,2048]{1,0:T(8,128)(2,1)S(1)} %pad_maximum_fusion.14), channel_id=1, source_target_pairs={{0,24},{1,25},{2,26},{3,27},{4,28},{5,29},{6,30},{7,31},{8,16},{9,... | collective-permute-start | bytes 393224 | tf_op jit(solution)/shard_map/ppermute | solution.py:606
  (34 other events, 309.1 us)
Sparse Core Ops, SparseCore 0:
  13.4 153.5 all-gather.1
